TPU v7x, 256 devices: a whole 4x4x8 slice. The times are simulated.
256 devices in a mesh: dp: 16 (over z, core), seq: 16 (over y, x).
Axes of the slice: x: 4, y: 4, z: 8, core: 2. Of those that a mesh axis runs over, the one named last changes fastest.
Arguments:
- queries: bfloat16 [16, 4096, 1024], P('dp', 'seq'), may hold values from -80 to 80
- keys: bfloat16 [16, 4096, 1024], P('dp', 'seq'), may hold values from -80 to 80
- values: bfloat16 [16, 4096, 1024], P('dp', 'seq'), may hold values from -12 to 12
- upstream: bfloat16 [16, 4096, 1024], P('dp', 'seq'), may hold values from -6 to 6
- w_out: bfloat16 [1024, 1024], replicated, may hold values from -0.1875 to 0.1875
- key_blocks: int32 [16, 32, 16], P('dp'), may hold values from 0 to 31, as said below
- block_counts: int32 [16, 32], P('dp'), may hold values from 1 to 16, as said below
Outputs:
- mixed: bfloat16 [16, 4096, 1024], P('dp', 'seq')
- grad_q: bfloat16 [16, 4096, 1024], P('dp', 'seq')
- grad_k: bfloat16 [16, 4096, 1024], P('dp', 'seq')
- grad_v: bfloat16 [16, 4096, 1024], P('dp', 'seq')
- grad_wo: float32 [1024, 1024], P('seq', 'dp')
Inputs may be any that keep to these rules, and one draw needn't show every extreme that they name: `key_blocks`: row b of a sequence's lists holds 16 distinct block numbers, the first of them b itself; entries past block_counts are valid numbers and are not used. `block_counts`: every sequence has a query block with exactly 16 used entries.
All inputs are finite; a program needn't handle non-finite values.
Results may differ from a plain program's by a relative error of at most 0.039.
Values may be sent and summed in bfloat16 or wider, within the bound.
No kernel may reach another device: no remote copies, remote signals or barrier semaphores. Data moves between devices by JAX's collectives and lax.ppermute only.
A program may use at most 128 MiB of HBM per device.

v0:
```python
import math

import jax
import jax.numpy as jnp
from jax import lax
from jax.sharding import PartitionSpec as P

HEADS = 16


blocks_per_step = 4


def product(form, left, right):
    return jnp.einsum(form, left, right, preferred_element_type=jnp.float32)


def inner_rows(left, right):
    return lax.dot_general(
        left, right, (((0,), (0,)), ((), ())), preferred_element_type=jnp.float32
    )


def block_attention(head_q, head_k, head_v, head_g, key_lists, key_counts):
    node_count, head_count, head_width = head_q.shape
    block_count, listed = key_lists.shape
    block_rows = node_count // block_count
    steps_count = block_count // blocks_per_step
    score_scale = 1.0 / math.sqrt(head_width)
    query_groups = head_q.reshape(steps_count, blocks_per_step, block_rows, head_count, head_width)
    grad_groups = head_g.reshape(steps_count, blocks_per_step, block_rows, head_count, head_width)
    key_table = head_k.reshape(block_count, block_rows, head_count, head_width)
    value_table = head_v.reshape(block_count, block_rows, head_count, head_width)
    list_groups = key_lists.reshape(steps_count, blocks_per_step, listed)
    count_groups = key_counts.reshape(steps_count, blocks_per_step)
    slot_index = jnp.arange(listed, dtype=jnp.int32)

    def one_step(accumulated, inputs):
        key_acc, value_acc = accumulated
        query_part, grad_part, list_part, count_part = inputs
        keys_near = key_table[list_part]
        values_near = value_table[list_part]
        scores = product("gqnd,gjknd->gnqjk", query_part, keys_near) * score_scale
        usable = (slot_index[None, :] < count_part[:, None])[:, None, None, :, None]
        scores = jnp.where(usable, scores, -jnp.inf)
        highest = jnp.max(scores, axis=(3, 4), keepdims=True)
        raised = jnp.exp(scores - highest)
        probability = raised / jnp.sum(raised, axis=(3, 4), keepdims=True)
        weights = probability.astype(jnp.bfloat16)
        attended = product("gnqjk,gjknd->gqnd", weights, values_near).astype(jnp.bfloat16)
        row_delta = jnp.sum(grad_part.astype(jnp.float32) * attended.astype(jnp.float32), axis=3)
        grad_scores = product("gqnd,gjknd->gnqjk", grad_part, values_near)
        shifted = grad_scores - jnp.transpose(row_delta, (0, 2, 1))[:, :, :, None, None]
        grad_logits = (probability * shifted).astype(jnp.bfloat16)
        grad_query = (product("gnqjk,gjknd->gqnd", grad_logits, keys_near) * score_scale).astype(
            jnp.bfloat16
        )
        key_terms = product("gnqjk,gqnd->gjknd", grad_logits, query_part) * score_scale
        value_terms = product("gnqjk,gqnd->gjknd", weights, grad_part)
        flat_list = list_part.reshape(-1)
        key_acc = key_acc.at[flat_list].add(
            key_terms.reshape(-1, block_rows, head_count, head_width)
        )
        value_acc = value_acc.at[flat_list].add(
            value_terms.reshape(-1, block_rows, head_count, head_width)
        )
        return ((key_acc, value_acc), (attended, grad_query))

    empty = jnp.zeros((block_count, block_rows, head_count, head_width), jnp.float32)
    (key_acc, value_acc), (attended, grad_query) = lax.scan(
        one_step, (empty, empty), (query_groups, grad_groups, list_groups, count_groups)
    )
    shape = (node_count, head_count, head_width)
    return (
        attended.reshape(shape),
        grad_query.reshape(shape),
        key_acc.astype(jnp.bfloat16).reshape(shape),
        value_acc.astype(jnp.bfloat16).reshape(shape),
    )


def project_back(up_rows, w_out):
    return lax.dot_general(
        up_rows, w_out, (((1,), (1,)), ((), ())), preferred_element_type=jnp.float32
    ).astype(jnp.bfloat16)


def local(queries, keys, values, upstream, w_out, key_blocks, block_counts):
    local_rows = queries.shape[1]
    width = queries.shape[2]
    head_width = width // HEADS
    up_rows = upstream[0]

    def split_heads(array):
        return array.reshape(local_rows, HEADS, head_width)

    query_heads = split_heads(queries[0])
    key_heads = split_heads(keys[0])
    value_heads = split_heads(values[0])
    grad_att = project_back(up_rows, w_out)
    head_q, head_k, head_v, head_g = (
        lax.all_to_all(query_heads, "seq", split_axis=1, concat_axis=0, tiled=True),
        lax.all_to_all(key_heads, "seq", split_axis=1, concat_axis=0, tiled=True),
        lax.all_to_all(value_heads, "seq", split_axis=1, concat_axis=0, tiled=True),
        lax.all_to_all(split_heads(grad_att), "seq", split_axis=1, concat_axis=0, tiled=True),
    )
    attended, grad_query, grad_key, grad_value = block_attention(
        head_q, head_k, head_v, head_g, key_blocks[0], block_counts[0]
    )
    node_att, node_gq, node_gk, node_gv = (
        lax.all_to_all(attended, "seq", split_axis=0, concat_axis=1, tiled=True),
        lax.all_to_all(grad_query, "seq", split_axis=0, concat_axis=1, tiled=True),
        lax.all_to_all(grad_key, "seq", split_axis=0, concat_axis=1, tiled=True),
        lax.all_to_all(grad_value, "seq", split_axis=0, concat_axis=1, tiled=True),
    )
    att_nodes = node_att.reshape(local_rows, width)
    mixed = jnp.dot(att_nodes, w_out, preferred_element_type=jnp.float32).astype(jnp.bfloat16)
    factor = 1.0 / math.sqrt(lax.axis_size("dp") * lax.axis_size("seq") * local_rows)
    summed = lax.psum_scatter(
        inner_rows(att_nodes, up_rows), "seq", scatter_dimension=0, tiled=True
    )
    grad_wo = lax.psum_scatter(summed, "dp", scatter_dimension=1, tiled=True)
    full_shape = (1, local_rows, width)
    return (
        mixed.reshape(full_shape),
        node_gq.reshape(full_shape),
        node_gk.reshape(full_shape),
        node_gv.reshape(full_shape),
        grad_wo * factor,
    )


def solution(mesh):
    placed = (
        P("dp", "seq", None),
        P("dp", "seq", None),
        P("dp", "seq", None),
        P("dp", "seq", None),
        P(),
        P("dp", None, None),
        P("dp", None),
    )
    return jax.shard_map(
        local,
        mesh=mesh,
        in_specs=placed,
        out_specs=(
            P("dp", "seq", None),
            P("dp", "seq", None),
            P("dp", "seq", None),
            P("dp", "seq", None),
            P("seq", "dp"),
        ),
        check_vma=False,
    )
```

profile of v0, /device:TPU:1, one launch (start us, length us, event | category | flops | bytes accessed | tf_op | source)
XLA Modules:
  0.0 668.8 jit_solution(1037919634291692953)
XLA Ops:
  9.4 7.6 %all-to-all-start.1 = ((bf16[256,16,64]{0,2,1:T(8,128)(2,1)}), bf16[256,16,64]{0,2,1:T(8,128)(2,1)S(1)}, u32[]{:S(2)}, u32[]{:S(2)}) async-start(bf16[256,16,64]{0,2,1:T(8,128)(2,1)} %bitcast.4), calls=%async_computation.1 | async-start | bytes 1048576 | tf_op jit(solution)/shard_map/all_to_all | solution.py:103
  19.0 8.5 %all-to-all-done.1 = bf16[256,16,64]{0,2,1:T(8,128)(2,1)S(1)} async-done(((bf16[256,16,64]{0,2,1:T(8,128)(2,1)}), bf16[256,16,64]{0,2,1:T(8,128)(2,1)S(1)}, u32[]{:S(2)}, u32[]{:S(2)}) %all-to-all-start.1) | async-done | bytes 524320 | tf_op jit(solution)/shard_map/all_to_all | solution.py:103
  27.5 3.7 all-to-all-start.3
  35.8 5.0 all-to-all-done.3
  40.9 4.2 all-to-all-start.2
  47.1 7.0 %all-to-all-done.2 = bf16[256,16,64]{0,2,1:T(8,128)(2,1)} async-done(((bf16[256,16,64]{0,2,1:T(8,128)(2,1)}), bf16[256,16,64]{0,2,1:T(8,128)(2,1)}, u32[]{:S(2)}, u32[]{:S(2)}) %all-to-all-start.2) | async-done | bytes 524320 | tf_op jit(solution)/shard_map/all_to_all | solution.py:105
  54.1 4.2 all-to-all-start
  71.0 336.6 %while.17 = (s32[]{:T(128)}, f32[32,128,1,64]{1,3,0,2:T(8,128)S(1)}, f32[32,128,1,64]{1,3,0,2:T(8,128)}, bf16[8,4,128,1,64]{2,4,1,3,0:T(8,128)(2,1)}, bf16[8,4,1...) while((s32[]{:T(128)}, ...), condition=%wide.region_6.7_spmd.clone, body=%wide.region_0.6_spmd.clone.sunk | while | flops 832274368 | bytes 99450016 | solution.py:70
  81.1 10.4 %scatter_fusion.1 = f32[32,128,64]{1,2,0:T(8,128)} fusion(f32[32,128,64]{1,2,0:T(8,128)} %bitcast.241, s32[64]{0:T(128)S(1)} %fusion.62, f32[64,128,64]{1,2,0:T(8,128)} %bitcast.248), kind=kCustom, calls=%fused_computation.3.clone.clone.1 | custom fusion | flops 524288 | bytes 6291712 | tf_op jit(solution)/shard_map/while/body/eval_jaxpr/scatter-add | solution.py:64
  94.1 4.0 fusion.66
  102.4 7.0 %scatter_fusion = f32[32,128,64]{1,2,0:T(8,128)S(1)} fusion(f32[32,128,64]{1,2,0:T(8,128)S(1)} %bitcast.239, s32[64]{0:T(128)S(1)} %fusion.62, f32[64,128,64]{1,2,0:T(8,128)} %bitcast.243), kind=kCustom, calls=%fused_computation.2.clone.clone.1 | custom fusion | flops 524288 | bytes 6291712 | tf_op jit(solution)/shard_map/while/body/eval_jaxpr/scatter-add | solution.py:61
  109.4 3.1 fusion.68
  123.2 10.3 %scatter_fusion.1 = f32[32,128,64]{1,2,0:T(8,128)} fusion(f32[32,128,64]{1,2,0:T(8,128)} %bitcast.241, s32[64]{0:T(128)S(1)} %fusion.62, f32[64,128,64]{1,2,0:T(8,128)} %bitcast.248), kind=kCustom, calls=%fused_computation.3.clone.clone.1 | custom fusion | flops 524288 | bytes 6291712 | tf_op jit(solution)/shard_map/while/body/eval_jaxpr/scatter-add | solution.py:64
  136.2 4.0 fusion.66
  144.5 7.0 %scatter_fusion = f32[32,128,64]{1,2,0:T(8,128)S(1)} fusion(f32[32,128,64]{1,2,0:T(8,128)S(1)} %bitcast.239, s32[64]{0:T(128)S(1)} %fusion.62, f32[64,128,64]{1,2,0:T(8,128)} %bitcast.243), kind=kCustom, calls=%fused_computation.2.clone.clone.1 | custom fusion | flops 524288 | bytes 6291712 | tf_op jit(solution)/shard_map/while/body/eval_jaxpr/scatter-add | solution.py:61
  151.5 3.1 fusion.68
  165.2 10.4 %scatter_fusion.1 = f32[32,128,64]{1,2,0:T(8,128)} fusion(f32[32,128,64]{1,2,0:T(8,128)} %bitcast.241, s32[64]{0:T(128)S(1)} %fusion.62, f32[64,128,64]{1,2,0:T(8,128)} %bitcast.248), kind=kCustom, calls=%fused_computation.3.clone.clone.1 | custom fusion | flops 524288 | bytes 6291712 | tf_op jit(solution)/shard_map/while/body/eval_jaxpr/scatter-add | solution.py:64
  178.3 4.0 fusion.66
  186.6 7.0 %scatter_fusion = f32[32,128,64]{1,2,0:T(8,128)S(1)} fusion(f32[32,128,64]{1,2,0:T(8,128)S(1)} %bitcast.239, s32[64]{0:T(128)S(1)} %fusion.62, f32[64,128,64]{1,2,0:T(8,128)} %bitcast.243), kind=kCustom, calls=%fused_computation.2.clone.clone.1 | custom fusion | flops 524288 | bytes 6291712 | tf_op jit(solution)/shard_map/while/body/eval_jaxpr/scatter-add | solution.py:61
  193.6 3.1 fusion.68
  207.3 10.4 %scatter_fusion.1 = f32[32,128,64]{1,2,0:T(8,128)} fusion(f32[32,128,64]{1,2,0:T(8,128)} %bitcast.241, s32[64]{0:T(128)S(1)} %fusion.62, f32[64,128,64]{1,2,0:T(8,128)} %bitcast.248), kind=kCustom, calls=%fused_computation.3.clone.clone.1 | custom fusion | flops 524288 | bytes 6291712 | tf_op jit(solution)/shard_map/while/body/eval_jaxpr/scatter-add | solution.py:64
  220.4 4.0 fusion.66
  228.7 7.0 %scatter_fusion = f32[32,128,64]{1,2,0:T(8,128)S(1)} fusion(f32[32,128,64]{1,2,0:T(8,128)S(1)} %bitcast.239, s32[64]{0:T(128)S(1)} %fusion.62, f32[64,128,64]{1,2,0:T(8,128)} %bitcast.243), kind=kCustom, calls=%fused_computation.2.clone.clone.1 | custom fusion | flops 524288 | bytes 6291712 | tf_op jit(solution)/shard_map/while/body/eval_jaxpr/scatter-add | solution.py:61
  235.7 3.1 fusion.68
  249.4 10.3 %scatter_fusion.1 = f32[32,128,64]{1,2,0:T(8,128)} fusion(f32[32,128,64]{1,2,0:T(8,128)} %bitcast.241, s32[64]{0:T(128)S(1)} %fusion.62, f32[64,128,64]{1,2,0:T(8,128)} %bitcast.248), kind=kCustom, calls=%fused_computation.3.clone.clone.1 | custom fusion | flops 524288 | bytes 6291712 | tf_op jit(solution)/shard_map/while/body/eval_jaxpr/scatter-add | solution.py:64
  262.5 4.0 fusion.66
  270.7 7.0 %scatter_fusion = f32[32,128,64]{1,2,0:T(8,128)S(1)} fusion(f32[32,128,64]{1,2,0:T(8,128)S(1)} %bitcast.239, s32[64]{0:T(128)S(1)} %fusion.62, f32[64,128,64]{1,2,0:T(8,128)} %bitcast.243), kind=kCustom, calls=%fused_computation.2.clone.clone.1 | custom fusion | flops 524288 | bytes 6291712 | tf_op jit(solution)/shard_map/while/body/eval_jaxpr/scatter-add | solution.py:61
  277.7 3.1 fusion.68
  291.5 10.4 %scatter_fusion.1 = f32[32,128,64]{1,2,0:T(8,128)} fusion(f32[32,128,64]{1,2,0:T(8,128)} %bitcast.241, s32[64]{0:T(128)S(1)} %fusion.62, f32[64,128,64]{1,2,0:T(8,128)} %bitcast.248), kind=kCustom, calls=%fused_computation.3.clone.clone.1 | custom fusion | flops 524288 | bytes 6291712 | tf_op jit(solution)/shard_map/while/body/eval_jaxpr/scatter-add | solution.py:64
  304.5 4.0 fusion.66
  312.8 7.0 %scatter_fusion = f32[32,128,64]{1,2,0:T(8,128)S(1)} fusion(f32[32,128,64]{1,2,0:T(8,128)S(1)} %bitcast.239, s32[64]{0:T(128)S(1)} %fusion.62, f32[64,128,64]{1,2,0:T(8,128)} %bitcast.243), kind=kCustom, calls=%fused_computation.2.clone.clone.1 | custom fusion | flops 524288 | bytes 6291712 | tf_op jit(solution)/shard_map/while/body/eval_jaxpr/scatter-add | solution.py:61
  319.8 3.1 fusion.68
  333.6 10.3 %scatter_fusion.1 = f32[32,128,64]{1,2,0:T(8,128)} fusion(f32[32,128,64]{1,2,0:T(8,128)} %bitcast.241, s32[64]{0:T(128)S(1)} %fusion.62, f32[64,128,64]{1,2,0:T(8,128)} %bitcast.248), kind=kCustom, calls=%fused_computation.3.clone.clone.1 | custom fusion | flops 524288 | bytes 6291712 | tf_op jit(solution)/shard_map/while/body/eval_jaxpr/scatter-add | solution.py:64
  346.6 4.0 fusion.66
  354.9 7.0 %scatter_fusion = f32[32,128,64]{1,2,0:T(8,128)S(1)} fusion(f32[32,128,64]{1,2,0:T(8,128)S(1)} %bitcast.239, s32[64]{0:T(128)S(1)} %fusion.62, f32[64,128,64]{1,2,0:T(8,128)} %bitcast.243), kind=kCustom, calls=%fused_computation.2.clone.clone.1 | custom fusion | flops 524288 | bytes 6291712 | tf_op jit(solution)/shard_map/while/body/eval_jaxpr/scatter-add | solution.py:61
  361.9 3.1 fusion.68
  375.6 10.3 %scatter_fusion.1 = f32[32,128,64]{1,2,0:T(8,128)} fusion(f32[32,128,64]{1,2,0:T(8,128)} %bitcast.241, s32[64]{0:T(128)S(1)} %fusion.62, f32[64,128,64]{1,2,0:T(8,128)} %bitcast.248), kind=kCustom, calls=%fused_computation.3.clone.clone.1 | custom fusion | flops 524288 | bytes 6291712 | tf_op jit(solution)/shard_map/while/body/eval_jaxpr/scatter-add | solution.py:64
  388.7 4.0 fusion.66
  397.0 7.0 %scatter_fusion = f32[32,128,64]{1,2,0:T(8,128)S(1)} fusion(f32[32,128,64]{1,2,0:T(8,128)S(1)} %bitcast.239, s32[64]{0:T(128)S(1)} %fusion.62, f32[64,128,64]{1,2,0:T(8,128)} %bitcast.243), kind=kCustom, calls=%fused_computation.2.clone.clone.1 | custom fusion | flops 524288 | bytes 6291712 | tf_op jit(solution)/shard_map/while/body/eval_jaxpr/scatter-add | solution.py:61
  404.0 3.1 fusion.68
  410.1 6.9 %reshape.327 = bf16[4096,1,64]{2,1,0:T(2,128)(2,1)} reshape(bf16[8,4,128,1,64]{4,2,1,0,3:T(8,128)(2,1)} %copy.99) | data formatting | bytes 1048576 | tf_op jit(solution)/shard_map/reshape | solution.py:75
  417.4 24.6 %reduce.9 = bf16[4096,64]{1,0:T(8,128)(2,1)} reduce(bf16[4096,1,64]{2,1,0:T(2,128)(2,1)} %reshape.327, bf16[]{:T(256)} %broadcast.127), dimensions={1}, to_apply=%reshape.327.reduce_sub_computation | reduce | bytes 1048578 | tf_op jit(solution)/shard_map/reshape | solution.py:75
  442.0 3.0 reshape.342
  445.0 15.8 %all_to_all.120 = bf16[16,2,8192]{2,1,0:T(2,128)(2,1)} all-to-all(bf16[16,2,8192]{2,1,0:T(2,128)(2,1)} %reshape.342), channel_id=1, replica_groups=mesh['dp'=16,'seq'=16] {'seq'}, dimensions={0} | all-to-all | bytes 1048576 | tf_op jit(solution)/shard_map/all_to_all | solution.py:111
  460.8 5.5 reshape.343
  466.3 5.2 copy.73
  473.7 3.7 fusion.24
  480.6 7.0 %reshape.329 = bf16[4096,1,64]{2,1,0:T(2,128)(2,1)} reshape(bf16[32,128,1,64]{3,1,0,2:T(8,128)(2,1)} %copy.101) | data formatting | bytes 1048576 | tf_op jit(solution)/shard_map/reshape | solution.py:77
  487.6 24.5 %reduce.11 = bf16[4096,64]{1,0:T(8,128)(2,1)} reduce(bf16[4096,1,64]{2,1,0:T(2,128)(2,1)} %reshape.329, bf16[]{:T(256)} %broadcast.127), dimensions={1}, to_apply=%reshape.329.reduce_sub_computation | reduce | bytes 1048578 | tf_op jit(solution)/shard_map/reshape | solution.py:77
  512.1 3.0 reshape.346
  515.1 4.5 all-to-all-start.6
  522.0 3.2 reshape.330
  525.2 23.5 %reduce.12 = bf16[4096,64]{1,0:T(8,128)(2,1)S(1)} reduce(bf16[4096,1,64]{2,1,0:T(2,128)(2,1)} %reshape.330, bf16[]{:T(256)} %broadcast.127), dimensions={1}, to_apply=%reshape.330.reduce_sub_computation | reduce | bytes 1048578 | tf_op jit(solution)/shard_map/reshape | solution.py:78
  550.1 7.0 %all-to-all-start.7 = ((bf16[16,2,8192]{2,1,0:T(2,128)(2,1)}), bf16[16,2,8192]{2,1,0:T(2,128)(2,1)}, u32[]{:S(2)}, u32[]{:S(2)}) async-start(bf16[16,2,8192]{2,1,0:T(2,128)(2,1)} %reshape.348), calls=%async_computation.7 | async-start | bytes 1048576 | tf_op jit(solution)/shard_map/all_to_all | solution.py:114
  558.7 3.2 reshape.328
  561.9 23.5 %reduce.10 = bf16[4096,64]{1,0:T(8,128)(2,1)S(1)} reduce(bf16[4096,1,64]{2,1,0:T(2,128)(2,1)} %reshape.328, bf16[]{:T(256)} %broadcast.127), dimensions={1}, to_apply=%reshape.328.reduce_sub_computation | reduce | bytes 1048578 | tf_op jit(solution)/shard_map/reshape | solution.py:76
  586.9 6.7 %all-to-all-start.5 = ((bf16[16,2,8192]{2,1,0:T(2,128)(2,1)}), bf16[16,2,8192]{2,1,0:T(2,128)(2,1)S(1)}, u32[]{:S(2)}, u32[]{:S(2)}) async-start(bf16[16,2,8192]{2,1,0:T(2,128)(2,1)} %reshape.344), calls=%async_computation.5 | async-start | bytes 1048576 | tf_op jit(solution)/shard_map/all_to_all | solution.py:112
  595.7 5.5 reshape.347
  601.2 4.6 copy.81
  607.1 5.5 reshape.349
  612.6 4.6 copy.85
  618.5 3.6 reshape.345
  622.1 4.6 copy.77
  629.5 30.7 %reduce-scatter.7.cloned.1.call-done = f32[64,64]{1,0:T(8,128)} async-done(((f32[1024,64]{1,0:T(8,128)}), f32[64,64]{1,0:T(8,128)}) %reduce-scatter.7.cloned.1.call-update) | async-done | bytes 16400
  (260 shorter events, 188.3 us)
Async XLA Ops:
  7.2 24.0 %copy-start = (bf16[1024,1024]{1,0:T(8,128)(2,1)S(1)}, bf16[1024,1024]{1,0:T(8,128)(2,1)}, u32[]{:S(2)}) copy-start(bf16[1024,1024]{1,0:T(8,128)(2,1)} %param.13) | copy-start | bytes 6291460
  9.4 18.1 %all-to-all-start.1 = ((bf16[256,16,64]{0,2,1:T(8,128)(2,1)}), bf16[256,16,64]{0,2,1:T(8,128)(2,1)S(1)}, u32[]{:S(2)}, u32[]{:S(2)}) async-start(bf16[256,16,64]{0,2,1:T(8,128)(2,1)} %bitcast.4), calls=%async_computation.1 | async-start | bytes 1048576 | tf_op jit(solution)/shard_map/all_to_all | solution.py:103
  27.5 32.0 %copy-start.9 = (s32[1,32]{1,0:T(1,128)S(1)}, s32[1,32]{1,0:T(1,128)}, u32[]{:S(2)}) copy-start(s32[1,32]{1,0:T(1,128)} %param.15) | copy-start | bytes 388
  27.5 32.7 %copy-start.8 = (s32[1,32,16]{1,2,0:T(8,128)S(1)}, s32[1,32,16]{1,2,0:T(8,128)}, u32[]{:S(2)}) copy-start(s32[1,32,16]{1,2,0:T(8,128)} %param.14) | copy-start | bytes 6148
  27.5 13.4 %all-to-all-start.3 = ((bf16[256,16,64]{0,2,1:T(8,128)(2,1)}), bf16[256,16,64]{0,2,1:T(8,128)(2,1)S(1)}, u32[]{:S(2)}, u32[]{:S(2)}) async-start(bf16[256,16,64]{0,2,1:T(8,128)(2,1)} %bitcast.261), calls=%async_computation.3 | async-start | bytes 1048576 | tf_op jit(solution)/shard_map/all_to_all | solution.py:104
  40.9 13.3 %all-to-all-start.2 = ((bf16[256,16,64]{0,2,1:T(8,128)(2,1)}), bf16[256,16,64]{0,2,1:T(8,128)(2,1)}, u32[]{:S(2)}, u32[]{:S(2)}) async-start(bf16[256,16,64]{0,2,1:T(8,128)(2,1)} %bitcast.262), calls=%async_computation.2 | async-start | bytes 1048576 | tf_op jit(solution)/shard_map/all_to_all | solution.py:105
  54.1 13.5 %all-to-all-start = ((bf16[256,16,64]{0,2,1:T(8,128)(2,1)}), bf16[256,16,64]{0,2,1:T(8,128)(2,1)}, u32[]{:S(2)}, u32[]{:S(2)}) async-start(bf16[256,16,64]{0,2,1:T(8,128)(2,1)} %bitcast.260), calls=%async_computation | async-start | bytes 1048576 | tf_op jit(solution)/shard_map/all_to_all | solution.py:102
  58.4 535.3 %reduce-scatter.5.cloned.1.call-start = ((), (), s32[]{:S(2)}) async-start(), calls=%async_computation.10 | async-start | bytes 4456448 | tf_op jit(solution)/shard_map/reduce_scatter | solution.py:119
  77.3 3.6 copy-start.2
  94.1 4.0 copy-start.3
  94.1 4.0 copy-start.5
  100.3 2.2 copy-start.4
  119.4 3.6 copy-start.2
  136.2 4.0 copy-start.3
  136.2 4.0 copy-start.5
  142.3 2.2 copy-start.4
  161.5 3.6 copy-start.2
  178.3 4.0 copy-start.3
  178.3 4.0 copy-start.5
  184.4 2.2 copy-start.4
  203.6 3.6 copy-start.2
  220.4 4.0 copy-start.3
  220.4 4.0 copy-start.5
  226.5 2.2 copy-start.4
  245.7 3.6 copy-start.2
  262.5 4.0 copy-start.3
  262.5 4.0 copy-start.5
  268.6 2.2 copy-start.4
  287.7 3.6 copy-start.2
  304.5 4.0 copy-start.3
  304.5 4.0 copy-start.5
  310.7 2.2 copy-start.4
  329.8 3.6 copy-start.2
  346.6 4.0 copy-start.3
  346.6 4.0 copy-start.5
  352.7 2.2 copy-start.4
  371.9 3.6 copy-start.2
  388.7 4.0 copy-start.3
  388.7 4.0 copy-start.5
  394.8 2.2 copy-start.4
  472.9 0.8 copy-start.6
  480.6 38.9 %copy-start.1 = (f32[32,128,1,64]{1,3,0,2:T(8,128)S(1)}, f32[32,128,1,64]{1,3,0,2:T(8,128)}, u32[]{:S(2)}) copy-start(f32[32,128,1,64]{1,3,0,2:T(8,128)} %get-tuple-element.73) | copy-start | bytes 3145732
  515.1 35.0 %all-to-all-start.6 = ((bf16[16,2,8192]{2,1,0:T(2,128)(2,1)}), bf16[16,2,8192]{2,1,0:T(2,128)(2,1)}, u32[]{:S(2)}, u32[]{:S(2)}) async-start(bf16[16,2,8192]{2,1,0:T(2,128)(2,1)} %reshape.346), calls=%async_computation.6 | async-start | bytes 1048576 | tf_op jit(solution)/shard_map/all_to_all | solution.py:113
  550.1 36.7 %all-to-all-start.7 = ((bf16[16,2,8192]{2,1,0:T(2,128)(2,1)}), bf16[16,2,8192]{2,1,0:T(2,128)(2,1)}, u32[]{:S(2)}, u32[]{:S(2)}) async-start(bf16[16,2,8192]{2,1,0:T(2,128)(2,1)} %reshape.348), calls=%async_computation.7 | async-start | bytes 1048576 | tf_op jit(solution)/shard_map/all_to_all | solution.py:114
  586.9 31.6 %all-to-all-start.5 = ((bf16[16,2,8192]{2,1,0:T(2,128)(2,1)}), bf16[16,2,8192]{2,1,0:T(2,128)(2,1)S(1)}, u32[]{:S(2)}, u32[]{:S(2)}) async-start(bf16[16,2,8192]{2,1,0:T(2,128)(2,1)} %reshape.344), calls=%async_computation.5 | async-start | bytes 1048576 | tf_op jit(solution)/shard_map/all_to_all | solution.py:112
  593.6 66.6 %reduce-scatter.7.cloned.1.call-start = ((), (), s32[]{:S(2)}) async-start(), calls=%async_computation.11 | async-start | bytes 557056
  618.5 9.5 %copy-start.7 = (bf16[256,16,1,64]{0,3,1,2:T(8,128)(2,1)S(1)}, bf16[256,16,1,64]{0,3,1,2:T(8,128)(2,1)}, u32[]{:S(2)}) copy-start(bf16[256,16,1,64]{0,3,1,2:T(8,128)(2,1)} %copy-done.6) | copy-start | bytes 1572868
Sparse Core Ops, SparseCore 0:
  477.5 88.8 reduce-scatter.4
  597.1 63.0 reduce-scatter.6
where the time goes:
time: 681 us; the launch traced here: 669 us
  other arithmetic  247 us (36%)
  local copies, waits for them, and re-layouts  163 us (24%)
  matrix products  139 us (20%)
  waiting for transfers between devices  51.4 us (8%)
  starting transfers between devices  38.7 us (6%)
  blocking collectives  15.8 us (2%)
  between operations  14.6 us (2%)
    dot_general x48, matrix products, product(): return jnp.einsum(form, left, right, preferred_element_type=jnp.float32)  131 us
    scatter-add x8, other arithmetic, one_step(): value_acc.at[flat_list]  82.9 us
    scatter-add x8, other arithmetic, one_step(): key_acc.at[flat_list]  56 us
    unnamed x36, local copies, waits for them, and re-layouts  46.2 us
    unnamed x3, waiting for transfers between devices  30.8 us
    reshape x1, other arithmetic, block_attention(): attended.reshape(shape)  24.6 us
    reshape x1, other arithmetic, block_attention(): key_acc.astype(jnp.bfloat16).reshape(shape)  24.5 us
    reshape x1, other arithmetic, block_attention(): grad_query.reshape(shape)  23.5 us
  transfers between devices with their start and end apart: 9, of which 5 were waited for; matrix products, arithmetic and copies ran while one was open for 23% of the time, Pallas kernels for 0%

commit v1 on v0

v1 whole, which is shorter than its diff:
```python
import math

import jax
import jax.numpy as jnp
from jax import lax
from jax.experimental import pallas as pl
from jax.experimental.pallas import tpu as pltpu
from jax.sharding import PartitionSpec as P

HEADS = 16
HEAD_WIDTH = 64
BLOCK_ROWS = 128
LANES = 2 * HEAD_WIDTH
SLOTS_PER_STEP = 4
MASKED = -1e30
SCORE_SCALE = 1.0 / math.sqrt(HEAD_WIDTH)
EXP2_SCALE = SCORE_SCALE * math.log2(math.e)

VMEM_SPEC = pl.BlockSpec(memory_space=pltpu.VMEM)
SMEM_SPEC = pl.BlockSpec(memory_space=pltpu.SMEM)


def dot(left, right, contract):
    return lax.dot_general(
        left, right, (contract, ((), ())), preferred_element_type=jnp.float32
    )


def head_columns(head):
    return slice(head * HEAD_WIDTH, (head + 1) * HEAD_WIDTH)


def pair_columns(left_ref, right, out_ref):
    for head in range(HEADS):
        columns = head_columns(head)
        out_ref[head] = jnp.concatenate([left_ref[:, columns], right[:, columns]], axis=1)


def pack_keys_values(key_ref, value_ref, out_ref):
    pair_columns(key_ref, value_ref, out_ref)


def pack_queries_grads(query_ref, up_ref, wo_ref, out_ref):
    grad = dot(up_ref[...], wo_ref[...], ((1,), (1,))).astype(jnp.bfloat16)
    pair_columns(query_ref, grad, out_ref)


def attention_kernel(
    list_ref, count_ref, kv_ref, qg_ref, ga_ref, gkv_ref, kv_turned, score_buf, gkv_acc
):
    blocks = kv_ref.shape[0]
    group_rows = SLOTS_PER_STEP * BLOCK_ROWS
    lane = lax.broadcasted_iota(jnp.int32, (BLOCK_ROWS, LANES), 1)
    low = lane < HEAD_WIDTH

    def prepare(block, _):
        kv_turned[block] = kv_ref[block].T
        gkv_acc[block] = jnp.zeros((BLOCK_ROWS, LANES), jnp.float32)
        return 0

    lax.fori_loop(0, blocks, prepare, 0)

    def one_query_block(block, _):
        count = count_ref[block]
        groups = (count + SLOTS_PER_STEP - 1) // SLOTS_PER_STEP
        qg = qg_ref[block]
        zero = jnp.zeros_like(qg)
        qg_split = jnp.concatenate([jnp.where(low, qg, zero), jnp.where(low, zero, qg)], axis=0)

        def score_step(group, highest):
            for unit in range(SLOTS_PER_STEP):
                slot = group * SLOTS_PER_STEP + unit
                both = dot(kv_ref[list_ref[block, slot]], qg_split, ((1,), (1,)))
                scores = jnp.where(slot < count, both[:, :BLOCK_ROWS], MASKED)
                rows = pl.ds(pl.multiple_of(slot * BLOCK_ROWS, BLOCK_ROWS), BLOCK_ROWS)
                score_buf[rows, :BLOCK_ROWS] = scores
                score_buf[rows, BLOCK_ROWS:] = both[:, BLOCK_ROWS:]
                highest = jnp.maximum(highest, jnp.max(scores.reshape(-1, 8, BLOCK_ROWS), axis=0))
            return highest

        highest = lax.fori_loop(
            0, groups, score_step, jnp.full((8, BLOCK_ROWS), MASKED, jnp.float32)
        )
        highest = jnp.max(highest, axis=0, keepdims=True)

        def raise_step(group, sums):
            total, weighted = sums
            rows = pl.ds(pl.multiple_of(group * group_rows, group_rows), group_rows)
            raised = jnp.exp2((score_buf[rows, :BLOCK_ROWS] - highest) * EXP2_SCALE)
            score_buf[rows, :BLOCK_ROWS] = raised
            total = total + jnp.sum(raised.reshape(-1, 8, BLOCK_ROWS), axis=0)
            terms = raised * score_buf[rows, BLOCK_ROWS:]
            weighted = weighted + jnp.sum(terms.reshape(-1, 8, BLOCK_ROWS), axis=0)
            return total, weighted

        empty = jnp.zeros((8, BLOCK_ROWS), jnp.float32)
        total, weighted = lax.fori_loop(0, groups, raise_step, (empty, empty))
        inverse = 1.0 / jnp.sum(total, axis=0, keepdims=True)
        row_delta = jnp.sum(weighted, axis=0, keepdims=True) * inverse

        def grad_step(group, sums):
            grad_q, attended = sums
            for half in range(SLOTS_PER_STEP // 2):
                slot = group * SLOTS_PER_STEP + 2 * half
                rows = pl.ds(pl.multiple_of(slot * BLOCK_ROWS, 2 * BLOCK_ROWS), 2 * BLOCK_ROWS)
                first, second = list_ref[block, slot], list_ref[block, slot + 1]
                probability = score_buf[rows, :BLOCK_ROWS] * inverse
                logits = probability * (score_buf[rows, BLOCK_ROWS:] - row_delta)
                joined = jnp.concatenate([logits, probability], axis=1).astype(jnp.bfloat16)
                key_terms = dot(joined, qg_split, ((1,), (0,)))
                gkv_acc[first] += key_terms[:BLOCK_ROWS]
                gkv_acc[second] += key_terms[BLOCK_ROWS:]
                turned = jnp.concatenate([kv_turned[first], kv_turned[second]], axis=1)
                query_terms = dot(turned, joined, ((1,), (0,)))
                grad_q = grad_q + query_terms[:HEAD_WIDTH, :BLOCK_ROWS]
                attended = attended + query_terms[HEAD_WIDTH:, BLOCK_ROWS:]
            return grad_q, attended

        empty = jnp.zeros((HEAD_WIDTH, BLOCK_ROWS), jnp.float32)
        grad_q, attended = lax.fori_loop(0, groups, grad_step, (empty, empty))
        turned = jnp.concatenate([grad_q * SCORE_SCALE, attended], axis=0)
        ga_ref[block] = turned.T.astype(jnp.bfloat16)
        return 0

    lax.fori_loop(0, blocks, one_query_block, 0)

    scale = jnp.where(low, SCORE_SCALE, 1.0)

    def finish(block, _):
        gkv_ref[block] = (gkv_acc[block] * scale).astype(jnp.bfloat16)
        return 0

    lax.fori_loop(0, blocks, finish, 0)


def finish_kernel(
    core_ref, ga_ref, gkv_ref, up_ref, wo_ref, mixed_ref, gq_ref, gk_ref, gv_ref, keep_ref, send_ref
):
    attended = []
    for head in range(HEADS):
        columns = head_columns(head)
        gq_ref[:, columns] = ga_ref[head, :, :HEAD_WIDTH]
        gk_ref[:, columns] = gkv_ref[head, :, :HEAD_WIDTH]
        gv_ref[:, columns] = gkv_ref[head, :, HEAD_WIDTH:]
        attended.append(ga_ref[head, :, HEAD_WIDTH:])
    attended = jnp.concatenate(attended, axis=1)
    mixed_ref[...] = dot(attended, wo_ref[...], ((1,), (0,))).astype(jnp.bfloat16)
    pieces = up_ref.shape[1] // HEAD_WIDTH
    even = jnp.concatenate([up_ref[:, head_columns(i)] for i in range(0, pieces, 2)], axis=1)
    odd = jnp.concatenate([up_ref[:, head_columns(i)] for i in range(1, pieces, 2)], axis=1)
    first = core_ref[0] == 0
    own = jnp.where(first, even, odd)
    other = jnp.where(first, odd, even)
    keep_ref[...] = dot(attended, own, ((0,), (0,)))
    send_ref[...] = dot(attended, other, ((0,), (0,))).astype(jnp.bfloat16)


def local(queries, keys, values, upstream, w_out, key_blocks, block_counts):
    local_rows, width = queries.shape[1:]
    seq_size, dp_size = lax.axis_size("seq"), lax.axis_size("dp")
    blocks = block_counts.shape[1]
    node_count = local_rows * seq_size
    up_rows = upstream[0]
    packed = jax.ShapeDtypeStruct((HEADS, local_rows, LANES), jnp.bfloat16)
    by_block = (blocks, BLOCK_ROWS, LANES)
    params = pltpu.CompilerParams(vmem_limit_bytes=48 * 2**20)

    kv_send = pl.pallas_call(
        pack_keys_values,
        out_shape=packed,
        in_specs=[VMEM_SPEC] * 2,
        out_specs=VMEM_SPEC,
        compiler_params=params,
    )(keys[0], values[0])
    kv = lax.all_to_all(kv_send, "seq", split_axis=0, concat_axis=0, tiled=True)
    qg_send = pl.pallas_call(
        pack_queries_grads,
        out_shape=packed,
        in_specs=[VMEM_SPEC] * 3,
        out_specs=VMEM_SPEC,
        compiler_params=params,
    )(queries[0], up_rows, w_out)
    qg = lax.all_to_all(qg_send, "seq", split_axis=0, concat_axis=0, tiled=True)

    ga, gkv = pl.pallas_call(
        attention_kernel,
        out_shape=[jax.ShapeDtypeStruct(by_block, jnp.bfloat16)] * 2,
        in_specs=[SMEM_SPEC, SMEM_SPEC, VMEM_SPEC, VMEM_SPEC],
        out_specs=[VMEM_SPEC] * 2,
        scratch_shapes=[
            pltpu.VMEM((blocks, LANES, BLOCK_ROWS), jnp.bfloat16),
            pltpu.VMEM((key_blocks.shape[2] * BLOCK_ROWS, 2 * BLOCK_ROWS), jnp.float32),
            pltpu.VMEM(by_block, jnp.float32),
        ],
        compiler_params=params,
    )(key_blocks[0], block_counts[0], kv.reshape(by_block), qg.reshape(by_block))

    by_head = (HEADS, local_rows, LANES)
    ga = lax.all_to_all(ga.reshape(by_head), "seq", split_axis=0, concat_axis=0, tiled=True)
    gkv = lax.all_to_all(gkv.reshape(by_head), "seq", split_axis=0, concat_axis=0, tiled=True)

    core = lax.axis_index("dp") % 2
    half = width // 2
    rows = jax.ShapeDtypeStruct((local_rows, width), jnp.bfloat16)
    mixed, gq, gk, gv, keep, send = pl.pallas_call(
        finish_kernel,
        out_shape=[
            rows,
            rows,
            rows,
            rows,
            jax.ShapeDtypeStruct((width, half), jnp.float32),
            jax.ShapeDtypeStruct((width, half), jnp.bfloat16),
        ],
        in_specs=[SMEM_SPEC] + [VMEM_SPEC] * 4,
        out_specs=[VMEM_SPEC] * 6,
        compiler_params=params,
    )(core.reshape(1).astype(jnp.int32), ga, gkv, up_rows, w_out)

    other_core = [(i, i + 1 - 2 * (i % 2)) for i in range(dp_size)]
    chips = dp_size // 2
    same_core = [[2 * z + c for z in range(chips)] for c in range(2)]
    chip_sum = (keep + lax.ppermute(send, "dp", other_core).astype(jnp.float32)).astype(jnp.bfloat16)
    parts = lax.all_to_all(
        chip_sum.reshape(seq_size, width // seq_size, half), "seq", split_axis=0, concat_axis=0, tiled=True
    )
    seq_sum = jnp.sum(parts.astype(jnp.float32), axis=0).astype(jnp.bfloat16)
    seq_sum = jnp.swapaxes(seq_sum.reshape(width // seq_size, chips, half // chips), 0, 1)
    terms = lax.all_to_all(
        seq_sum, "dp", split_axis=0, concat_axis=0, axis_index_groups=same_core, tiled=True
    )
    factor = 1.0 / math.sqrt(dp_size * node_count)
    grad_wo = jnp.sum(terms.astype(jnp.float32), axis=0) * factor
    full_shape = (1, local_rows, width)
    return (
        mixed.reshape(full_shape),
        gq.reshape(full_shape),
        gk.reshape(full_shape),
        gv.reshape(full_shape),
        grad_wo,
    )


def solution(mesh):
    placed = (
        P("dp", "seq", None),
        P("dp", "seq", None),
        P("dp", "seq", None),
        P("dp", "seq", None),
        P(),
        P("dp", None, None),
        P("dp", None),
    )
    return jax.shard_map(
        local,
        mesh=mesh,
        in_specs=placed,
        out_specs=(
            P("dp", "seq", None),
            P("dp", "seq", None),
            P("dp", "seq", None),
            P("dp", "seq", None),
            P("seq", "dp"),
        ),
        check_vma=False,
    )
```

time: 681 us -> 192 us (0.28); the launches traced: 669 us -> 192 us
  other arithmetic: 247 us -> 1.15 us
  local copies, waits for them, and re-layouts: 163 us -> 4.22 us
  matrix products: 139 us -> 0 us
  Pallas kernels: 0 us -> 56.9 us
  blocking collectives: 15.8 us -> 46 us
  between operations: 14.6 us -> 0.78 us
    scatter-add x16 -> x0, other arithmetic: 139 us -> none  [the longest x8 82.9 us: one_step(): value_acc.at[flat_list]]
    dot_general x51 -> x0, matrix products: 139 us -> none  [the longest x48 131 us: product(): return jnp.einsum(form, left, right, preferred_element_type=jnp.float32)]
    reshape x4 -> x0, other arithmetic: 96 us -> none  [the longest x1 24.6 us: block_attention(): attended.reshape(shape)]
    pallas_call x0 -> x4, Pallas kernels: none -> 56.9 us  [the longest x1 49.5 us: local(): pl.pallas_call(attention_kernel, out_shape=[jax.ShapeDtypeStruct(by_block...]
    gather x16 -> x0, local copies, waits for them, and re-layouts: 43.4 us -> none  [the longest x8 21.8 us: one_step(): keys_near = key_table[list_part]]
    unnamed x36 -> x21, local copies, waits for them, and re-layouts: 46.2 us -> 4.07 us
    reshape x21 -> x1, local copies, waits for them, and re-layouts: 32.4 us -> 0.13 us  [local(): seq_sum.reshape(width // seq_size, chips, half // chips)]
    unnamed x3 -> x0, waiting for transfers between devices: 30.8 us -> none
  transfers between devices with their start and end apart: 9 -> 4, of which waited for: 5 -> 4; matrix products, arithmetic and copies ran while one was open for 23% -> 0% of each run, Pallas kernels for 0% -> 1%
where the time goes in v1:
time: 192 us
  Pallas kernels  56.9 us (30%)
  waiting for transfers between devices  49.9 us (26%)
  blocking collectives  46 us (24%)
  starting transfers between devices  32.9 us (17%)
  local copies, waits for them, and re-layouts  4.22 us (2%)
    pallas_call x1, Pallas kernels, local(): pl.pallas_call(attention_kernel, out_shape=[jax.ShapeDtypeStruct(by_block...  49.5 us
    all_to_all x1, blocking collectives, local(): lax.all_to_all(chip_sum.reshape(seq_size, width // seq_size, half), 'seq'...  19 us
    all_to_all x1, waiting for transfers between devices, local(): lax.all_to_all(ga.reshape(by_head), 'seq', split_axis=0, concat_axis=0, t...  18 us
    ppermute x1, starting transfers between devices, local(): lax.ppermute(send, 'dp', other_core).astype(jnp.float32)  17.4 us
    all_to_all x1, blocking collectives, local(): lax.all_to_all(gkv.reshape(by_head), 'seq', split_axis=0, concat_axis=0,...  16.6 us
    all_to_all x1, waiting for transfers between devices, local(): kv = lax.all_to_all(kv_send, 'seq', split_axis=0, concat_axis=0, tiled=True)  15 us
    all_to_all x1, waiting for transfers between devices, local(): qg = lax.all_to_all(qg_send, 'seq', split_axis=0, concat_axis=0, tiled=True)  14.6 us
    all_to_all x1, blocking collectives, local(): lax.all_to_all(seq_sum, 'dp', split_axis=0, concat_axis=0, axis_index_gro...  10.4 us
  transfers between devices with their start and end apart: 4, of which 4 were waited for; matrix products, arithmetic and copies ran while one was open for 0% of the time, Pallas kernels for 1%

profile of v1, /device:TPU:1, one launch (start us, length us, event | category | flops | bytes accessed | tf_op | source)
XLA Modules:
  0.0 191.8 jit_solution(11975559463583083924)
XLA Ops:
  0.6 0.0 copy-start
  0.6 1.6 copy-done
  2.2 0.0 copy-start.1
  2.2 1.0 copy-done.1
  3.3 0.0 copy-start.6
  3.3 1.0 copy-done.6
  4.3 1.8 shard_map.111
  6.1 0.0 copy-start.4
  6.1 0.0 copy-start.5
  6.1 7.7 %all-to-all-start.1 = ((bf16[16,256,128]{2,1,0:T(8,128)(2,1)}), bf16[16,256,128]{2,1,0:T(8,128)(2,1)S(1)}, u32[]{:S(2)}, u32[]{:S(2)}) async-start(bf16[16,256,128]{2,1,0:T(8,128)(2,1)} %shard_map.111), calls=%async_computation.1 | async-start | bytes 2097152 | tf_op jit(solution)/shard_map/all_to_all | solution.py:183
  13.9 0.0 copy-done.4
  13.9 0.0 copy-done.5
  13.9 0.0 copy-start.8
  13.9 0.0 copy-start.7
  13.9 1.3 shard_map.110
  15.2 14.6 %all-to-all-done.1 = bf16[16,256,128]{2,1,0:T(8,128)(2,1)S(1)} async-done(((bf16[16,256,128]{2,1,0:T(8,128)(2,1)}), bf16[16,256,128]{2,1,0:T(8,128)(2,1)S(1)}, u32[]{:S(2)}, u32[]{:S(2)}) %all-to-all-start.1) | async-done | bytes 1048608 | tf_op jit(solution)/shard_map/all_to_all | solution.py:183
  29.8 4.2 %all-to-all-start = ((bf16[16,256,128]{2,1,0:T(8,128)(2,1)}), bf16[16,256,128]{2,1,0:T(8,128)(2,1)S(1)}, u32[]{:S(2)}, u32[]{:S(2)}) async-start(bf16[16,256,128]{2,1,0:T(8,128)(2,1)} %shard_map.110), calls=%async_computation | async-start | bytes 2097152 | tf_op jit(solution)/shard_map/all_to_all | solution.py:175
  34.1 0.0 copy-done.8
  34.1 0.1 copy.14
  34.1 15.0 %all-to-all-done = bf16[16,256,128]{2,1,0:T(8,128)(2,1)S(1)} async-done(((bf16[16,256,128]{2,1,0:T(8,128)(2,1)}), bf16[16,256,128]{2,1,0:T(8,128)(2,1)S(1)}, u32[]{:S(2)}, u32[]{:S(2)}) %all-to-all-start) | async-done | bytes 1048608 | tf_op jit(solution)/shard_map/all_to_all | solution.py:175
  49.1 0.0 copy-done.7
  49.1 49.5 %shard_map.112 = (bf16[32,128,128]{2,1,0:T(8,128)(2,1)S(1)}, bf16[32,128,128]{2,1,0:T(8,128)(2,1)S(1)}) custom-call(s32[32,16]{1,0:T(8,128)S(1)} %bitcast.26, s32[32]{0:T(128)S(1)} %bitcast.27, bf16[32,128,128]{2,1,0:T(8,128)(2,1)S(1)} %bitcast.18, bf16[32,128,128]{2,1,0:T(8,128)(2,1)S(1)} %bitcast.17), custom_call_target="tpu_custom_call" | custom-call | tf_op jit(solution)/shard_map/pallas_call | solution.py:185
  98.6 0.0 copy-start.3
  98.6 0.0 copy-start.2
  98.6 16.6 %all_to_all.30.gkv_ref = bf16[16,256,128]{2,1,0:T(8,128)(2,1)S(1)} all-to-all(bf16[16,256,128]{2,1,0:T(8,128)(2,1)S(1)} %bitcast.22), channel_id=1, replica_groups=mesh['dp'=16,'seq'=16] {'seq'}, dimensions={0} | all-to-all | bytes 2097152 | tf_op jit(solution)/shard_map/all_to_all | solution.py:200
  115.3 0.0 copy-done.3
  115.3 3.7 %all-to-all-start.2 = ((bf16[16,256,128]{2,1,0:T(8,128)(2,1)}), bf16[16,256,128]{2,1,0:T(8,128)(2,1)S(1)}, u32[]{:S(2)}, u32[]{:S(2)}) async-start(bf16[16,256,128]{2,1,0:T(8,128)(2,1)} %bitcast.21), calls=%async_computation.2 | async-start | bytes 2097152 | tf_op jit(solution)/shard_map/all_to_all | solution.py:199
  118.9 18.0 %all-to-all-done.2.ga_ref = bf16[16,256,128]{2,1,0:T(8,128)(2,1)S(1)} async-done(((bf16[16,256,128]{2,1,0:T(8,128)(2,1)}), bf16[16,256,128]{2,1,0:T(8,128)(2,1)S(1)}, u32[]{:S(2)}, u32[]{:S(2)}) %all-to-all-start.2) | async-done | bytes 1048608 | tf_op jit(solution)/shard_map/all_to_all | solution.py:199
  136.9 0.0 copy-done.2
  136.9 4.3 %shard_map.113 = (bf16[256,1024]{1,0:T(8,128)(2,1)}, bf16[256,1024]{1,0:T(8,128)(2,1)}, bf16[256,1024]{1,0:T(8,128)(2,1)}, bf16[256,1024]{1,0:T(8,128)(2,1)}, f3...) custom-call(s32[1]{0:T(128)} %bitcast.core_ref, bf16[16,256,128]{2,1,0:T(8,128)(2,1)S(1)} %all-to-all-done.2.ga_ref, ...), custom_call_target="tpu_custom_call" | custom-call | tf_op jit(solution)/shard_map/pallas_call | solution.py:205
  141.2 17.4 %collective-permute-start = (bf16[1024,512]{1,0:T(8,128)(2,1)S(1)}, bf16[1024,512]{1,0:T(8,128)(2,1)S(1)}, u32[]{:S(2)}, u32[]{:S(2)}) collective-permute-start(bf16[1024,512]{1,0:T(8,128)(2,1)S(1)} %get-tuple-element.20), channel_id=1, source_target_pairs={{0,16},{16,0},{32,48},{48,32},{64,80},{80,64},{96,112},{112,96},{1... | collective-permute-start | bytes 3145736 | tf_op jit(solution)/shard_map/ppermute | solution.py:223
  158.6 2.3 %collective-permute-done = bf16[1024,512]{1,0:T(8,128)(2,1)S(1)} collective-permute-done((bf16[1024,512]{1,0:T(8,128)(2,1)S(1)}, bf16[1024,512]{1,0:T(8,128)(2,1)S(1)}, u32[]{:S(2)}, u32[]{:S(2)}) %collective-permute-start) | collective-permute-done | bytes 1048608 | tf_op jit(solution)/shard_map/ppermute | solution.py:223
  160.8 0.3 add_convert_fusion
  161.2 19.0 %all_to_all.31 = bf16[16,64,512]{2,1,0:T(8,128)(2,1)S(1)} all-to-all(bf16[16,64,512]{2,1,0:T(8,128)(2,1)S(1)} %bitcast.28), channel_id=1, replica_groups=mesh['dp'=16,'seq'=16] {'seq'}, dimensions={0} | all-to-all | bytes 2097152 | tf_op jit(solution)/shard_map/all_to_all | solution.py:224
  180.2 0.1 reduce_sum.21
  180.4 0.1 reshape.53
  180.5 0.2 reshape.54
  180.7 10.4 %all_to_all.32 = bf16[8,2,2048]{2,1,0:T(2,128)(2,1)S(1)} all-to-all(bf16[8,2,2048]{2,1,0:T(2,128)(2,1)S(1)} %reshape.54), channel_id=1, replica_groups={{0,32,64,96,128,160,192,224},{16,48,80,112,144,176,208,240},{1,33,65,97..., dimensions={0} | all-to-all | bytes 131072 | tf_op jit(solution)/shard_map/all_to_all | solution.py:229
  191.0 0.1 reshape.55
  191.2 0.6 broadcast_multiply_fusion
  (2 shorter events, 0.1 us)
Async XLA Ops:
  0.6 1.6 copy-start
  2.2 1.0 copy-start.1
  3.3 1.0 copy-start.6
  6.1 7.7 %copy-start.4 = (bf16[1,256,1024]{2,1,0:T(8,128)(2,1)S(1)}, bf16[1,256,1024]{2,1,0:T(8,128)(2,1)}, u32[]{:S(2)}) copy-start(bf16[1,256,1024]{2,1,0:T(8,128)(2,1)} %param.8) | copy-start | bytes 1572868
  6.1 7.7 %copy-start.5 = (bf16[1,256,1024]{2,1,0:T(8,128)(2,1)S(1)}, bf16[1,256,1024]{2,1,0:T(8,128)(2,1)}, u32[]{:S(2)}) copy-start(bf16[1,256,1024]{2,1,0:T(8,128)(2,1)} %param.9) | copy-start | bytes 1572868
  6.1 23.7 %all-to-all-start.1 = ((bf16[16,256,128]{2,1,0:T(8,128)(2,1)}), bf16[16,256,128]{2,1,0:T(8,128)(2,1)S(1)}, u32[]{:S(2)}, u32[]{:S(2)}) async-start(bf16[16,256,128]{2,1,0:T(8,128)(2,1)} %shard_map.111), calls=%async_computation.1 | async-start | bytes 2097152 | tf_op jit(solution)/shard_map/all_to_all | solution.py:183
  13.9 20.2 %copy-start.8 = (s32[1,32,16]{1,2,0:T(8,128)S(1)}, s32[1,32,16]{1,2,0:T(8,128)}, u32[]{:S(2)}) copy-start(s32[1,32,16]{1,2,0:T(8,128)} %param.12) | copy-start | bytes 6148
  13.9 35.2 %copy-start.7 = (s32[1,32]{1,0:T(1,128)S(1)}, s32[1,32]{1,0:T(1,128)}, u32[]{:S(2)}) copy-start(s32[1,32]{1,0:T(1,128)} %param.13) | copy-start | bytes 388
  29.8 19.3 %all-to-all-start = ((bf16[16,256,128]{2,1,0:T(8,128)(2,1)}), bf16[16,256,128]{2,1,0:T(8,128)(2,1)S(1)}, u32[]{:S(2)}, u32[]{:S(2)}) async-start(bf16[16,256,128]{2,1,0:T(8,128)(2,1)} %shard_map.110), calls=%async_computation | async-start | bytes 2097152 | tf_op jit(solution)/shard_map/all_to_all | solution.py:175
  98.6 16.7 %copy-start.3 = (bf16[32,128,128]{2,1,0:T(8,128)(2,1)}, bf16[32,128,128]{2,1,0:T(8,128)(2,1)S(1)}, u32[]{:S(2)}) copy-start(bf16[32,128,128]{2,1,0:T(8,128)(2,1)S(1)} %get-tuple-element.13) | copy-start | bytes 3145732
  98.6 38.3 %copy-start.2 = (bf16[1,256,1024]{2,1,0:T(8,128)(2,1)S(1)}, bf16[1,256,1024]{2,1,0:T(8,128)(2,1)}, u32[]{:S(2)}) copy-start(bf16[1,256,1024]{2,1,0:T(8,128)(2,1)} %param.10) | copy-start | bytes 1572868
  115.3 21.6 %all-to-all-start.2 = ((bf16[16,256,128]{2,1,0:T(8,128)(2,1)}), bf16[16,256,128]{2,1,0:T(8,128)(2,1)S(1)}, u32[]{:S(2)}, u32[]{:S(2)}) async-start(bf16[16,256,128]{2,1,0:T(8,128)(2,1)} %bitcast.21), calls=%async_computation.2 | async-start | bytes 2097152 | tf_op jit(solution)/shard_map/all_to_all | solution.py:199
  141.2 19.6 %collective-permute-start = (bf16[1024,512]{1,0:T(8,128)(2,1)S(1)}, bf16[1024,512]{1,0:T(8,128)(2,1)S(1)}, u32[]{:S(2)}, u32[]{:S(2)}) collective-permute-start(bf16[1024,512]{1,0:T(8,128)(2,1)S(1)} %get-tuple-element.20), channel_id=1, source_target_pairs={{0,16},{16,0},{32,48},{48,32},{64,80},{80,64},{96,112},{112,96},{1... | collective-permute-start | bytes 3145736 | tf_op jit(solution)/shard_map/ppermute | solution.py:223

commit v2 on v0

v2 whole, which is shorter than its diff:
```python
import functools
import math

import jax
import jax.numpy as jnp
from jax import lax
from jax.experimental import pallas as pl
from jax.experimental.pallas import tpu as pltpu
from jax.sharding import PartitionSpec as P

HEADS = 16
HEAD_WIDTH = 64
BLOCK_ROWS = 128
LANES = 2 * HEAD_WIDTH
FORWARD_TILE = 4
BACKWARD_TILE = 2
SLOT_STEP = 2
FIRST_TILES = 4
MASKED = -1e30
SCORE_SCALE = 1.0 / math.sqrt(HEAD_WIDTH)
EXP2_SCALE = SCORE_SCALE * math.log2(math.e)

VMEM_SPEC = pl.BlockSpec(memory_space=pltpu.VMEM)
SMEM_SPEC = pl.BlockSpec(memory_space=pltpu.SMEM)


def dot(left, right, contract):
    return lax.dot_general(
        left, right, (contract, ((), ())), preferred_element_type=jnp.float32
    )


def call(kernel, name, outs, in_specs, scratch=(), flops=0, **kwargs):
    return pl.pallas_call(
        kernel,
        out_shape=outs,
        in_specs=in_specs,
        out_specs=[VMEM_SPEC] * len(outs),
        scratch_shapes=list(scratch),
        compiler_params=pltpu.CompilerParams(vmem_limit_bytes=24 * 2**20),
        cost_estimate=pl.CostEstimate(flops=flops, bytes_accessed=4 * 2**20, transcendentals=0),
        name=name,
        **kwargs,
    )


def pack_kernel(query_ref, key_ref, value_ref, up_ref, wo_ref, out_ref):
    grads = dot(up_ref[...], wo_ref[...], ((1,), (1,))).astype(jnp.bfloat16)
    heads_here = out_ref.shape[0]
    for head in range(heads_here):
        columns = slice(head * HEAD_WIDTH, (head + 1) * HEAD_WIDTH)
        kv = jnp.concatenate([key_ref[:, columns], value_ref[:, columns]], axis=1)
        qg = jnp.concatenate([query_ref[:, columns], grads[:, columns]], axis=1)
        for block in range(out_ref.shape[1]):
            rows = slice(block * BLOCK_ROWS, (block + 1) * BLOCK_ROWS)
            out_ref[head, block, :BLOCK_ROWS] = kv[rows]
            out_ref[head, block, BLOCK_ROWS:] = qg[rows]


def pack(queries, keys, values, up_rows, w_out):
    rows, width = queries.shape
    blocks = rows // BLOCK_ROWS
    steps = 4
    columns = width // steps
    part = pl.BlockSpec((rows, columns), lambda i: (0, i))
    return pl.pallas_call(
        pack_kernel,
        grid=(steps,),
        out_shape=jax.ShapeDtypeStruct((HEADS, blocks, 2 * BLOCK_ROWS, LANES), jnp.bfloat16),
        in_specs=[
            part,
            part,
            part,
            pl.BlockSpec((rows, width), lambda i: (0, 0)),
            pl.BlockSpec((columns, width), lambda i: (i, 0)),
        ],
        out_specs=pl.BlockSpec(
            (HEADS // steps, blocks, 2 * BLOCK_ROWS, LANES), lambda i: (i, 0, 0, 0)
        ),
        compiler_params=pltpu.CompilerParams(vmem_limit_bytes=60 * 2**20),
        name="pack",
    )(queries, keys, values, up_rows, w_out)


def for_tiles(tiles, tile_blocks, listed, order_ref, count_ref, process):
    def one_tile(tile, _):
        members = [order_ref[tile * tile_blocks + i] for i in range(tile_blocks)]
        steps = (count_ref[members[0]] + SLOT_STEP - 1) // SLOT_STEP
        sizes = range(SLOT_STEP, listed + 1, SLOT_STEP)
        lax.switch(steps - 1, [functools.partial(process, members, size) for size in sizes])
        return 0

    lax.fori_loop(*tiles, one_tile, 0)


def by_fours(blocks, body):
    def four(index, _):
        for unit in range(4):
            body(4 * index + unit)
        return 0

    lax.fori_loop(0, blocks // 4, four, 0)


def forward_kernel(list_ref, count_ref, order_ref, in_ref, att_ref, stat_ref, turned, *score_bufs):
    blocks, listed = list_ref.shape
    low = lax.broadcasted_iota(jnp.int32, (LANES, BLOCK_ROWS), 0) < HEAD_WIDTH

    def turn(block):
        turned[block] = in_ref[block, :BLOCK_ROWS].T[HEAD_WIDTH:]

    by_fours(blocks, turn)

    def process(members, slots):
        qg_turned = [in_ref[block, BLOCK_ROWS:].T for block in members]
        queries = [jnp.where(low, array, jnp.zeros_like(array)) for array in qg_turned]
        near = [[list_ref[block, slot] for slot in range(slots)] for block in members]
        highest = []
        for i, block in enumerate(members):
            rows = jnp.concatenate([in_ref[key, :BLOCK_ROWS] for key in near[i]], axis=0)
            scores = dot(rows, queries[i], ((1,), (0,)))
            top = jnp.full((8, BLOCK_ROWS), MASKED, jnp.float32)
            for slot in range(slots):
                here = slice(slot * BLOCK_ROWS, (slot + 1) * BLOCK_ROWS)
                part = jnp.where(slot < count_ref[block], scores[here], MASKED)
                score_bufs[i][here] = part
                top = jnp.maximum(top, jnp.max(part.reshape(-1, 8, BLOCK_ROWS), axis=0))
            highest.append(jnp.max(top, axis=0, keepdims=True))
        for i, block in enumerate(members):
            part = score_bufs[i][: slots * BLOCK_ROWS]
            raised = jnp.exp2((part - highest[i]) * EXP2_SCALE)
            total = jnp.sum(raised, axis=0, keepdims=True)
            flat = jnp.concatenate([turned[key] for key in near[i]], axis=1)
            sums = dot(flat, raised.astype(jnp.bfloat16), ((1,), (0,)))
            attended = (sums * (1.0 / total)).astype(jnp.bfloat16)
            att_ref[block] = attended
            grads = qg_turned[i][HEAD_WIDTH:].astype(jnp.float32)
            delta = jnp.sum(attended.astype(jnp.float32) * grads, axis=0, keepdims=True)
            stat_ref[block, 0:1] = highest[i] + jnp.log2(total) * (1.0 / EXP2_SCALE)
            stat_ref[block, 1:2] = delta

    for_tiles(
        (0, blocks // FORWARD_TILE), FORWARD_TILE, listed, order_ref, count_ref, process
    )


def backward_kernel(tiles, first, list_ref, count_ref, order_ref, in_ref, stat_ref, *refs):
    if first:
        out_ref, acc_ref, turned = refs
    else:
        gq_before, acc_before, out_ref, turned, acc_ref = refs
    blocks, listed = list_ref.shape
    low_lanes = lax.broadcasted_iota(jnp.int32, (BLOCK_ROWS, LANES), 1) < HEAD_WIDTH
    low_rows = lax.broadcasted_iota(jnp.int32, (LANES, BLOCK_ROWS), 0) < HEAD_WIDTH

    def prepare(block):
        turned[block] = in_ref[block, :BLOCK_ROWS].T[:HEAD_WIDTH]
        if first:
            acc_ref[block] = jnp.zeros((BLOCK_ROWS, LANES), jnp.float32)
        else:
            acc_ref[block] = acc_before[block]
            out_ref[block, :HEAD_WIDTH] = gq_before[block]

    by_fours(blocks, prepare)

    def process(members, slots):
        for block in members:
            qg = in_ref[block, BLOCK_ROWS:]
            flat = qg.T
            zero = jnp.zeros_like(qg)
            across = jnp.concatenate(
                [jnp.where(low_rows, flat, zero), jnp.where(low_rows, zero, flat)], axis=1
            )
            down = jnp.concatenate(
                [jnp.where(low_lanes, qg, zero), jnp.where(low_lanes, zero, qg)], axis=0
            )
            top, delta = stat_ref[block, 0:1], stat_ref[block, 1:2]
            near = [list_ref[block, slot] for slot in range(slots)]
            rows = jnp.concatenate([in_ref[key, :BLOCK_ROWS] for key in near], axis=0)
            both = dot(rows, across, ((1,), (0,)))
            joined = []
            for slot in range(slots):
                part = both[slot * BLOCK_ROWS : (slot + 1) * BLOCK_ROWS]
                probability = jnp.exp2((part[:, :BLOCK_ROWS] - top) * EXP2_SCALE)
                probability = jnp.where(slot < count_ref[block], probability, 0.0)
                logits = probability * (part[:, BLOCK_ROWS:] - delta)
                joined.append(
                    jnp.concatenate(
                        [logits.astype(jnp.bfloat16), probability.astype(jnp.bfloat16)], axis=1
                    )
                )
            joined = jnp.concatenate(joined, axis=0)
            key_terms = dot(joined, down, ((1,), (0,)))
            for slot, key in enumerate(near):
                acc_ref[key] += key_terms[slot * BLOCK_ROWS : (slot + 1) * BLOCK_ROWS]
            flat = jnp.concatenate([turned[key] for key in near], axis=1)
            grads = dot(flat, joined[:, :BLOCK_ROWS], ((1,), (0,)))
            out_ref[block, :HEAD_WIDTH] = (grads * SCORE_SCALE).astype(jnp.bfloat16)

    for_tiles(tiles, BACKWARD_TILE, listed, order_ref, count_ref, process)
    if first:
        return
    scale = jnp.where(low_lanes, SCORE_SCALE, 1.0)

    def finish(block):
        out_ref[block, HEAD_WIDTH:] = (acc_ref[block] * scale).astype(jnp.bfloat16)

    by_fours(blocks, finish)


def weight_grad_kernel(core_ref, att_ref, up_ref, keep_ref, send_ref):
    attended = attended_columns(att_ref)
    pieces = up_ref.shape[1] // HEAD_WIDTH

    def every_other(start):
        return jnp.concatenate(
            [up_ref[:, i * HEAD_WIDTH : (i + 1) * HEAD_WIDTH] for i in range(start, pieces, 2)],
            axis=1,
        )

    even, odd = every_other(0), every_other(1)
    first = core_ref[0] == 0
    send_ref[...] = dot(attended, jnp.where(first, odd, even), ((1,), (0,))).astype(jnp.bfloat16)
    keep_ref[...] = dot(attended, jnp.where(first, even, odd), ((1,), (0,)))


def attended_columns(att_ref):
    heads, blocks = att_ref.shape[:2]
    return jnp.concatenate(
        [
            jnp.concatenate([att_ref[head, block] for head in range(heads)], axis=0)
            for block in range(blocks)
        ],
        axis=1,
    )


def mixed_kernel(att_ref, wo_ref, mixed_ref):
    attended = attended_columns(att_ref).T
    mixed_ref[...] = dot(attended, wo_ref[...], ((1,), (0,))).astype(jnp.bfloat16)


def unpack_kernel(in_ref, gq_ref, gk_ref, gv_ref):
    blocks = in_ref.shape[1]
    low = lax.broadcasted_iota(jnp.int32, (BLOCK_ROWS, LANES), 1) < HEAD_WIDTH
    for block in range(blocks):
        rows = slice(block * BLOCK_ROWS, (block + 1) * BLOCK_ROWS)
        for head in range(0, HEADS, 2):
            columns = slice(head * HEAD_WIDTH, (head + 2) * HEAD_WIDTH)
            flat = jnp.concatenate([in_ref[head + i, block, :HEAD_WIDTH] for i in range(2)], axis=0)
            gq_ref[rows, columns] = flat.T
            one, two = (in_ref[head + i, block, HEAD_WIDTH:] for i in range(2))
            gk_ref[rows, columns] = jnp.concatenate(
                [one[:, :HEAD_WIDTH], two[:, :HEAD_WIDTH]], axis=1
            )
            gv_ref[rows, columns] = jnp.concatenate(
                [one[:, HEAD_WIDTH:], two[:, HEAD_WIDTH:]], axis=1
            )


def by_falling_count(counts):
    index = jnp.arange(counts.shape[0], dtype=jnp.int32)
    place = -counts * counts.shape[0] + index
    rank = jnp.sum((place[None, :] < place[:, None]).astype(jnp.int32), axis=1)
    return jnp.sum(jnp.where(rank[None, :] == index[:, None], index[None, :], 0), axis=1)


def exchange(array):
    return lax.all_to_all(array, "seq", split_axis=0, concat_axis=0, tiled=True)


def local(queries, keys, values, upstream, w_out, key_blocks, block_counts):
    local_rows, width = queries.shape[1:]
    seq_size, dp_size = lax.axis_size("seq"), lax.axis_size("dp")
    lists, counts = key_blocks[0], block_counts[0]
    blocks, listed = lists.shape
    near_blocks = local_rows // BLOCK_ROWS
    up_rows = upstream[0]
    bf16, f32 = jnp.bfloat16, jnp.float32
    shape = jax.ShapeDtypeStruct
    smem, vmem = SMEM_SPEC, VMEM_SPEC

    packed = exchange(pack(queries[0], keys[0], values[0], up_rows, w_out))
    packed = packed.reshape(blocks, 2 * BLOCK_ROWS, LANES)
    lists, counts, order = lax.optimization_barrier((lists, counts, by_falling_count(counts)))
    listing = (lists, counts, order)
    turned = pltpu.VMEM((blocks, HEAD_WIDTH, BLOCK_ROWS), bf16)
    acc = (blocks, BLOCK_ROWS, LANES)
    half_turned = shape((blocks, HEAD_WIDTH, BLOCK_ROWS), bf16)

    attended, stats = call(
        forward_kernel,
        "forward",
        [half_turned, shape((blocks, 8, BLOCK_ROWS), f32)],
        [smem] * 3 + [vmem],
        [turned] + [pltpu.VMEM((listed * BLOCK_ROWS, BLOCK_ROWS), f32)] * FORWARD_TILE,
        flops=10 * 10**9,
    )(*listing, packed)

    attended = exchange(attended.reshape(seq_size, near_blocks, HEAD_WIDTH, BLOCK_ROWS))
    first = call(
        functools.partial(backward_kernel, (0, FIRST_TILES), True),
        "backward_first",
        [half_turned, shape(acc, f32)],
        [smem] * 3 + [vmem] * 2,
        [turned],
        flops=10 * 10**9,
    )(*listing, packed, stats)

    attended, first = lax.optimization_barrier((attended, first))
    half = width // 2
    core = (lax.axis_index("dp") % 2).reshape(1).astype(jnp.int32)
    keep, send = call(
        weight_grad_kernel,
        "weight_grad",
        [shape((width, half), f32), shape((width, half), bf16)],
        [smem] + [vmem] * 2,
        flops=10**9,
    )(core, attended, up_rows)
    other_core = [(i, i + 1 - 2 * (i % 2)) for i in range(dp_size)]
    received = lax.ppermute(send, "dp", other_core)
    chip_sum = (keep + received.astype(f32)).astype(bf16)

    chip_sum, first, attended = lax.optimization_barrier((chip_sum, first, attended))
    parts = exchange(chip_sum.reshape(seq_size, width // seq_size, half))
    (outgoing,) = call(
        functools.partial(backward_kernel, (FIRST_TILES, blocks // BACKWARD_TILE), False),
        "backward_second",
        [shape((blocks, HEAD_WIDTH + BLOCK_ROWS, LANES), bf16)],
        [smem] * 3 + [vmem] * 4,
        [turned, pltpu.VMEM(acc, f32)],
        flops=15 * 10**9,
    )(*listing, packed, stats, *first)

    parts, outgoing = lax.optimization_barrier((parts, outgoing))
    seq_sum = jnp.sum(parts.astype(f32), axis=0).astype(bf16)
    incoming = exchange(
        outgoing.reshape(seq_size, near_blocks, HEAD_WIDTH + BLOCK_ROWS, LANES)
    )
    chips = dp_size // 2
    same_core = [[2 * z + c for z in range(chips)] for c in range(2)]
    seq_sum = jnp.swapaxes(seq_sum.reshape(width // seq_size, chips, half // chips), 0, 1)
    seq_sum, incoming = lax.optimization_barrier((seq_sum, incoming))
    terms = lax.all_to_all(
        seq_sum, "dp", split_axis=0, concat_axis=0, axis_index_groups=same_core, tiled=True
    )
    factor = 1.0 / math.sqrt(dp_size * local_rows * seq_size)
    grad_wo = jnp.sum(terms.astype(f32), axis=0) * factor

    rows = shape((local_rows, width), bf16)
    (mixed,) = call(mixed_kernel, "mixed", [rows], [vmem] * 2, flops=10**9)(attended, w_out)
    gq, gk, gv = call(unpack_kernel, "unpack", [rows] * 3, [vmem])(incoming)
    full_shape = (1, local_rows, width)
    return (
        mixed.reshape(full_shape),
        gq.reshape(full_shape),
        gk.reshape(full_shape),
        gv.reshape(full_shape),
        grad_wo,
    )


def solution(mesh):
    nodes = P("dp", "seq", None)
    return jax.shard_map(
        local,
        mesh=mesh,
        in_specs=(nodes, nodes, nodes, nodes, P(), P("dp", None, None), P("dp", None)),
        out_specs=(nodes, nodes, nodes, nodes, P("seq", "dp")),
        check_vma=False,
    )
```

time: 681 us -> 152 us (0.22); the launches traced: 669 us -> 152 us
  other arithmetic: 247 us -> 3.7 us
  local copies, waits for them, and re-layouts: 163 us -> 7.62 us
  matrix products: 139 us -> 0 us
  Pallas kernels: 0 us -> 42 us
  blocking collectives: 15.8 us -> 0 us
  between operations: 14.6 us -> 0.8 us
    scatter-add x16 -> x0, other arithmetic: 139 us -> none  [the longest x8 82.9 us: one_step(): value_acc.at[flat_list]]
    dot_general x51 -> x0, matrix products: 139 us -> none  [the longest x48 131 us: product(): return jnp.einsum(form, left, right, preferred_element_type=jnp.float32)]
    reshape x4 -> x0, other arithmetic: 96 us -> none  [the longest x1 24.6 us: block_attention(): attended.reshape(shape)]
    gather x16 -> x0, local copies, waits for them, and re-layouts: 43.4 us -> none  [the longest x8 21.8 us: one_step(): keys_near = key_table[list_part]]
    pallas_call x0 -> x7, Pallas kernels: none -> 42 us  [the longest x1 13.3 us: local(): call(functools.partial(backward_kernel, (FIRST_TILES, blocks // BACKWARD_...]
    unnamed x36 -> x21, local copies, waits for them, and re-layouts: 46.2 us -> 7.47 us
    reshape x21 -> x1, local copies, waits for them, and re-layouts: 32.4 us -> 0.13 us  [local(): seq_sum.reshape(width // seq_size, chips, half // chips)]
    unnamed x3 -> x0, waiting for transfers between devices: 30.8 us -> none
  transfers between devices with their start and end apart: 9 -> 6, of which waited for: 5 -> 5; matrix products, arithmetic and copies ran while one was open for 23% -> 1% of each run, Pallas kernels for 0% -> 16%
where the time goes in v2:
time: 152 us
  waiting for transfers between devices  53.6 us (35%)
  starting transfers between devices  43.9 us (29%)
  Pallas kernels  42 us (28%)
  local copies, waits for them, and re-layouts  7.62 us (5%)
  other arithmetic  3.7 us (2%)
    all_to_all x4, waiting for transfers between devices, exchange(): return lax.all_to_all(array, 'seq', split_axis=0, concat_axis=0, tiled=True)  48.9 us
    all_to_all x4, starting transfers between devices, exchange(): return lax.all_to_all(array, 'seq', split_axis=0, concat_axis=0, tiled=True)  25.2 us
    all_to_all x1, starting transfers between devices, local(): lax.all_to_all(seq_sum, 'dp', split_axis=0, concat_axis=0, axis_index_gro...  15.5 us
    pallas_call x1, Pallas kernels, local(): call(functools.partial(backward_kernel, (FIRST_TILES, blocks // BACKWARD_...  13.3 us
    pallas_call x1, Pallas kernels, local(): call(forward_kernel, 'forward', [half_turned, shape((blocks, 8, BLOCK_ROW...  11.7 us
    pallas_call x1, Pallas kernels, local(): call(functools.partial(backward_kernel, (0, FIRST_TILES), True), 'backwar...  7.78 us
    unnamed x21, local copies, waits for them, and re-layouts  7.47 us
    pallas_call x1, Pallas kernels, pack(): pl.pallas_call(pack_kernel, grid=(steps,), out_shape=jax.ShapeDtypeStruct...  5.24 us
  transfers between devices with their start and end apart: 6, of which 5 were waited for; matrix products, arithmetic and copies ran while one was open for 1% of the time, Pallas kernels for 16%

profile of v2, /device:TPU:1, one launch (start us, length us, event | category | flops | bytes accessed | tf_op | source)
XLA Modules:
  0.0 151.6 jit_solution(2395717051030627393)
XLA Ops:
  0.6 5.2 %pack.1 = bf16[16,2,256,128]{3,2,1,0:T(8,128)(2,1)} custom-call(bf16[256,1024]{1,0:T(8,128)(2,1)} %bitcast.32, bf16[256,1024]{1,0:T(8,128)(2,1)} %bitcast.33, bf16[256,1024]{1,0:T(8,128)(2,1)} %bitcast.34, bf16[256,1024]{1,0:T(8,128)(2,1)} %bitcast.23, bf16[1024,1024]{1,0:T(8,128)(2,1)} %wo_ref.3), custom_call_target="tpu_custom_call" | custom-call | tf_op jit(solution)/shard_map/pack/pallas_call | solution.py:66
  5.9 0.0 copy-start.8
  5.9 0.0 copy-start.3
  5.9 7.7 %all-to-all-start = ((bf16[16,2,256,128]{3,2,1,0:T(8,128)(2,1)}), bf16[16,2,256,128]{3,2,1,0:T(8,128)(2,1)S(1)}, u32[]{:S(2)}, u32[]{:S(2)}) async-start(bf16[16,2,256,128]{3,2,1,0:T(8,128)(2,1)} %pack.1), calls=%async_computation | async-start | bytes 4194304 | tf_op jit(solution)/shard_map/all_to_all | solution.py:269
  13.6 0.0 copy-done.8
  13.6 0.1 copy.16
  13.7 0.0 copy-done.3
  13.7 0.2 convert_reduce_fusion.1
  13.9 0.1 select_reduce_fusion.order_ref
  14.0 30.1 %all-to-all-done = bf16[16,2,256,128]{3,2,1,0:T(8,128)(2,1)S(1)} async-done(((bf16[16,2,256,128]{3,2,1,0:T(8,128)(2,1)}), bf16[16,2,256,128]{3,2,1,0:T(8,128)(2,1)S(1)}, u32[]{:S(2)}, u32[]{:S(2)}) %all-to-all-start) | async-done | bytes 2097184 | tf_op jit(solution)/shard_map/all_to_all | solution.py:269
  44.1 11.7 %forward.1 = (bf16[32,64,128]{2,1,0:T(8,128)(2,1)}, f32[32,8,128]{2,1,0:T(8,128)S(1)}) custom-call(s32[32,16]{1,0:T(8,128)S(1)} %bitcast.25, s32[32]{0:T(128)S(1)} %bitcast.28, s32[32]{0:T(128)S(1)} %select_reduce_fusion.order_ref, bf16[32,256,128]{2,1,0:T(8,128)(2,1)S(1)} %bitcast.19), custom_call_target="tpu_custom_call" | custom-call | flops 10000000000 | bytes 4194304 | tf_op jit(solution)/shard_map/forward/pallas_call | solution.py:291
  55.8 4.3 %all-to-all-start.1 = ((bf16[16,2,64,128]{3,2,1,0:T(8,128)(2,1)}), bf16[16,2,64,128]{3,2,1,0:T(8,128)(2,1)S(1)}, u32[]{:S(2)}, u32[]{:S(2)}) async-start(bf16[16,2,64,128]{3,2,1,0:T(8,128)(2,1)} %bitcast.9), calls=%async_computation.1 | async-start | bytes 1048576 | tf_op jit(solution)/shard_map/all_to_all | solution.py:269
  60.1 0.0 copy-start.2
  60.1 7.8 %backward_first.1 = (bf16[32,64,128]{2,1,0:T(8,128)(2,1)S(1)}, f32[32,128,128]{2,1,0:T(8,128)S(1)}) custom-call(s32[32,16]{1,0:T(8,128)S(1)} %bitcast.26, s32[32]{0:T(128)S(1)} %bitcast.29, s32[32]{0:T(128)S(1)} %select_reduce_fusion.order_ref, bf16[32,256,128]{2,1,0:T(8,128)(2,1)S(1)} %bitcast.20, f32[32,8,128]{2,1,0:T(8,128)S(1)} %get-tuple-element.32.stat_ref), custom_call_target="tpu_custom_call" | custom-call | flops 10000000000 | bytes 4194304 | tf_op jit(solution)/shard_map/backward_first/pallas_call | solution.py:301
  67.9 0.0 copy-start.4
  67.9 1.3 copy-done.4
  69.2 0.0 copy-start.6
  69.2 0.8 copy-done.6
  70.0 0.0 all-to-all-done.1.att_ref
  70.0 0.0 copy-done.2
  70.0 0.9 weight_grad.1
  70.9 3.2 %collective-permute-start = (bf16[1024,512]{1,0:T(8,128)(2,1)S(1)}, bf16[1024,512]{1,0:T(8,128)(2,1)S(1)}, u32[]{:S(2)}, u32[]{:S(2)}) collective-permute-start(bf16[1024,512]{1,0:T(8,128)(2,1)S(1)} %get-tuple-element.37), channel_id=1, source_target_pairs={{0,16},{16,0},{32,48},{48,32},{64,80},{80,64},{96,112},{112,96},{1... | collective-permute-start | bytes 3145736 | tf_op jit(solution)/shard_map/ppermute | solution.py:321
  74.1 2.3 %collective-permute-done = bf16[1024,512]{1,0:T(8,128)(2,1)S(1)} collective-permute-done((bf16[1024,512]{1,0:T(8,128)(2,1)S(1)}, bf16[1024,512]{1,0:T(8,128)(2,1)S(1)}, u32[]{:S(2)}, u32[]{:S(2)}) %collective-permute-start) | collective-permute-done | bytes 1048608 | tf_op jit(solution)/shard_map/ppermute | solution.py:321
  76.4 1.4 add_convert_fusion
  77.8 0.0 copy-start.7
  77.8 6.9 %all-to-all-start.2 = ((bf16[16,64,512]{2,1,0:T(8,128)(2,1)}), bf16[16,64,512]{2,1,0:T(8,128)(2,1)}, u32[]{:S(2)}, u32[]{:S(2)}) async-start(bf16[16,64,512]{2,1,0:T(8,128)(2,1)} %bitcast.31), calls=%async_computation.2 | async-start | bytes 2097152 | tf_op jit(solution)/shard_map/all_to_all | solution.py:269
  84.7 0.0 copy-done.7
  84.7 0.0 copy-start.5
  84.7 1.6 %copy-done.5 = f32[32,128,128]{2,1,0:T(8,128)S(1)} copy-done((f32[32,128,128]{2,1,0:T(8,128)S(1)}, f32[32,128,128]{2,1,0:T(8,128)}, u32[]{:S(2)}) %copy-start.5) | copy-done | bytes 2097176
  86.3 13.3 %backward_second.1 = bf16[32,192,128]{2,1,0:T(8,128)(2,1)S(1)} custom-call(s32[32,16]{1,0:T(8,128)S(1)} %bitcast.27, s32[32]{0:T(128)S(1)} %bitcast.30, s32[32]{0:T(128)S(1)} %select_reduce_fusion.order_ref, bf16[32,256,128]{2,1,0:T(8,128)(2,1)S(1)} %bitcast.21, f32[32,8,128]{2,1,0:T(8,128)S(1)} %get-tuple-element.32.stat_ref, ...), custom_call_target="tpu_custom_call" | custom-call | flops 15000000512 | bytes 4194304 | tf_op jit(solution)/shard_map/backward_second/pallas_call | solution.py:326
  99.6 0.0 copy-start.1
  99.6 1.2 copy-done.1
  100.7 0.3 all-to-all-done.2
  101.1 6.3 %all-to-all-start.3 = ((bf16[16,2,192,128]{3,2,1,0:T(8,128)(2,1)}), bf16[16,2,192,128]{3,2,1,0:T(8,128)(2,1)S(1)}, u32[]{:S(2)}, u32[]{:S(2)}) async-start(bf16[16,2,192,128]{3,2,1,0:T(8,128)(2,1)} %bitcast.22), calls=%async_computation.3 | async-start | bytes 3145728 | tf_op jit(solution)/shard_map/all_to_all | solution.py:269
  107.3 1.4 reduce_sum.41
  108.7 0.1 reshape.57
  108.8 18.5 %all-to-all-done.3.in_ref = bf16[16,2,192,128]{3,2,1,0:T(8,128)(2,1)S(1)} async-done(((bf16[16,2,192,128]{3,2,1,0:T(8,128)(2,1)}), bf16[16,2,192,128]{3,2,1,0:T(8,128)(2,1)S(1)}, u32[]{:S(2)}, u32[]{:S(2)}) %all-to-all-start.3) | async-done | bytes 1572896 | tf_op jit(solution)/shard_map/all_to_all | solution.py:269
  127.3 0.8 reshape.62
  128.1 15.5 %all-to-all-start.4 = ((bf16[8,2,2048]{2,1,0:T(2,128)(2,1)}), bf16[8,2,2048]{2,1,0:T(2,128)(2,1)S(1)}, u32[]{:S(2)}, u32[]{:S(2)}) async-start(bf16[8,2,2048]{2,1,0:T(2,128)(2,1)} %reshape.62), calls=%async_computation.4 | async-start | bytes 131072 | tf_op jit(solution)/shard_map/all_to_all | solution.py:344
  143.6 0.0 copy-start
  143.7 1.6 %copy-done = bf16[1024,1024]{1,0:T(8,128)(2,1)S(1)} copy-done((bf16[1024,1024]{1,0:T(8,128)(2,1)S(1)}, bf16[1024,1024]{1,0:T(8,128)(2,1)}, u32[]{:S(2)}) %copy-start) | copy-done | bytes 2097176
  145.2 1.5 %mixed.1 = bf16[256,1024]{1,0:T(8,128)(2,1)} custom-call(bf16[16,2,64,128]{3,2,1,0:T(8,128)(2,1)S(1)} %all-to-all-done.1.att_ref, bf16[1024,1024]{1,0:T(8,128)(2,1)S(1)} %copy-done), custom_call_target="tpu_custom_call" | custom-call | flops 1000000000 | bytes 4194304 | tf_op jit(solution)/shard_map/mixed/pallas_call | solution.py:351
  146.8 1.6 %unpack.1 = (bf16[256,1024]{1,0:T(8,128)(2,1)}, bf16[256,1024]{1,0:T(8,128)(2,1)}, bf16[256,1024]{1,0:T(8,128)(2,1)}) custom-call(bf16[16,2,192,128]{3,2,1,0:T(8,128)(2,1)S(1)} %all-to-all-done.3.in_ref), custom_call_target="tpu_custom_call" | custom-call | bytes 4194304 | tf_op jit(solution)/shard_map/unpack/pallas_call | solution.py:352
  148.4 2.4 %all-to-all-done.4 = bf16[8,2,2048]{2,1,0:T(2,128)(2,1)S(1)} async-done(((bf16[8,2,2048]{2,1,0:T(2,128)(2,1)}), bf16[8,2,2048]{2,1,0:T(2,128)(2,1)S(1)}, u32[]{:S(2)}, u32[]{:S(2)}) %all-to-all-start.4) | async-done | bytes 65568 | tf_op jit(solution)/shard_map/all_to_all | solution.py:344
  150.8 0.1 reshape.63
  151.0 0.6 broadcast_multiply_fusion
  (4 shorter events, 0.1 us)
Async XLA Ops:
  5.9 7.7 %copy-start.8 = (s32[1,32,16]{1,2,0:T(8,128)S(1)}, s32[1,32,16]{1,2,0:T(8,128)}, u32[]{:S(2)}) copy-start(s32[1,32,16]{1,2,0:T(8,128)} %param.12) | copy-start | bytes 6148
  5.9 7.8 %copy-start.3 = (s32[1,32]{1,0:T(1,128)S(1)}, s32[1,32]{1,0:T(1,128)}, u32[]{:S(2)}) copy-start(s32[1,32]{1,0:T(1,128)} %param.13) | copy-start | bytes 388
  5.9 38.2 %all-to-all-start = ((bf16[16,2,256,128]{3,2,1,0:T(8,128)(2,1)}), bf16[16,2,256,128]{3,2,1,0:T(8,128)(2,1)S(1)}, u32[]{:S(2)}, u32[]{:S(2)}) async-start(bf16[16,2,256,128]{3,2,1,0:T(8,128)(2,1)} %pack.1), calls=%async_computation | async-start | bytes 4194304 | tf_op jit(solution)/shard_map/all_to_all | solution.py:269
  55.8 14.2 %all-to-all-start.1 = ((bf16[16,2,64,128]{3,2,1,0:T(8,128)(2,1)}), bf16[16,2,64,128]{3,2,1,0:T(8,128)(2,1)S(1)}, u32[]{:S(2)}, u32[]{:S(2)}) async-start(bf16[16,2,64,128]{3,2,1,0:T(8,128)(2,1)} %bitcast.9), calls=%async_computation.1 | async-start | bytes 1048576 | tf_op jit(solution)/shard_map/all_to_all | solution.py:269
  60.1 9.9 %copy-start.2 = (bf16[1,256,1024]{2,1,0:T(8,128)(2,1)S(1)}, bf16[1,256,1024]{2,1,0:T(8,128)(2,1)}, u32[]{:S(2)}) copy-start(bf16[1,256,1024]{2,1,0:T(8,128)(2,1)} %param.10) | copy-start | bytes 1572868
  67.9 1.3 copy-start.4
  69.2 0.8 copy-start.6
  70.9 5.5 %collective-permute-start = (bf16[1024,512]{1,0:T(8,128)(2,1)S(1)}, bf16[1024,512]{1,0:T(8,128)(2,1)S(1)}, u32[]{:S(2)}, u32[]{:S(2)}) collective-permute-start(bf16[1024,512]{1,0:T(8,128)(2,1)S(1)} %get-tuple-element.37), channel_id=1, source_target_pairs={{0,16},{16,0},{32,48},{48,32},{64,80},{80,64},{96,112},{112,96},{1... | collective-permute-start | bytes 3145736 | tf_op jit(solution)/shard_map/ppermute | solution.py:321
  77.8 6.9 %copy-start.7 = (bf16[32,64,128]{2,1,0:T(8,128)(2,1)S(1)}, bf16[32,64,128]{2,1,0:T(8,128)(2,1)}, u32[]{:S(2)}) copy-start(bf16[32,64,128]{2,1,0:T(8,128)(2,1)} %copy-done.6) | copy-start | bytes 1572868
  77.8 23.3 %all-to-all-start.2 = ((bf16[16,64,512]{2,1,0:T(8,128)(2,1)}), bf16[16,64,512]{2,1,0:T(8,128)(2,1)}, u32[]{:S(2)}, u32[]{:S(2)}) async-start(bf16[16,64,512]{2,1,0:T(8,128)(2,1)} %bitcast.31), calls=%async_computation.2 | async-start | bytes 2097152 | tf_op jit(solution)/shard_map/all_to_all | solution.py:269
  84.7 1.6 %copy-start.5 = (f32[32,128,128]{2,1,0:T(8,128)S(1)}, f32[32,128,128]{2,1,0:T(8,128)}, u32[]{:S(2)}) copy-start(f32[32,128,128]{2,1,0:T(8,128)} %copy-done.4) | copy-start | bytes 6291460
  99.6 1.2 copy-start.1
  101.1 26.3 %all-to-all-start.3 = ((bf16[16,2,192,128]{3,2,1,0:T(8,128)(2,1)}), bf16[16,2,192,128]{3,2,1,0:T(8,128)(2,1)S(1)}, u32[]{:S(2)}, u32[]{:S(2)}) async-start(bf16[16,2,192,128]{3,2,1,0:T(8,128)(2,1)} %bitcast.22), calls=%async_computation.3 | async-start | bytes 3145728 | tf_op jit(solution)/shard_map/all_to_all | solution.py:269
  128.1 22.7 %all-to-all-start.4 = ((bf16[8,2,2048]{2,1,0:T(2,128)(2,1)}), bf16[8,2,2048]{2,1,0:T(2,128)(2,1)S(1)}, u32[]{:S(2)}, u32[]{:S(2)}) async-start(bf16[8,2,2048]{2,1,0:T(2,128)(2,1)} %reshape.62), calls=%async_computation.4 | async-start | bytes 131072 | tf_op jit(solution)/shard_map/all_to_all | solution.py:344
  143.6 1.6 %copy-start = (bf16[1024,1024]{1,0:T(8,128)(2,1)S(1)}, bf16[1024,1024]{1,0:T(8,128)(2,1)}, u32[]{:S(2)}) copy-start(bf16[1024,1024]{1,0:T(8,128)(2,1)} %wo_ref.3) | copy-start | bytes 6291460

commit v3 on v2

--- a/solution.py
+++ b/solution.py
@@ -20,6 +20,7 @@
 SCORE_SCALE = 1.0 / math.sqrt(HEAD_WIDTH)
 EXP2_SCALE = SCORE_SCALE * math.log2(math.e)
 
+HBM_SPEC = pl.BlockSpec(memory_space=pltpu.HBM)
 VMEM_SPEC = pl.BlockSpec(memory_space=pltpu.VMEM)
 SMEM_SPEC = pl.BlockSpec(memory_space=pltpu.SMEM)
 
@@ -30,17 +31,16 @@
     )
 
 
-def call(kernel, name, outs, in_specs, scratch=(), flops=0, **kwargs):
+def call(kernel, name, outs, in_specs, scratch=(), flops=0, out_specs=None, vmem=24):
     return pl.pallas_call(
         kernel,
         out_shape=outs,
         in_specs=in_specs,
-        out_specs=[VMEM_SPEC] * len(outs),
+        out_specs=out_specs or [VMEM_SPEC] * len(outs),
         scratch_shapes=list(scratch),
-        compiler_params=pltpu.CompilerParams(vmem_limit_bytes=24 * 2**20),
+        compiler_params=pltpu.CompilerParams(vmem_limit_bytes=vmem * 2**20),
         cost_estimate=pl.CostEstimate(flops=flops, bytes_accessed=4 * 2**20, transcendentals=0),
         name=name,
-        **kwargs,
     )
 
 
@@ -60,7 +60,7 @@
 def pack(queries, keys, values, up_rows, w_out):
     rows, width = queries.shape
     blocks = rows // BLOCK_ROWS
-    steps = 4
+    steps = 2
     columns = width // steps
     part = pl.BlockSpec((rows, columns), lambda i: (0, i))
     return pl.pallas_call(
@@ -146,20 +146,19 @@
 
 def backward_kernel(tiles, first, list_ref, count_ref, order_ref, in_ref, stat_ref, *refs):
     if first:
-        out_ref, acc_ref, turned = refs
+        out_ref, acc_out, token_ref, turned, acc_ref, sems = refs
     else:
-        gq_before, acc_before, out_ref, turned, acc_ref = refs
+        gq_before, acc_in, out_hbm, token_ref, turned, acc_ref, acc_before, out_ref, sems = refs
+        fetch = pltpu.make_async_copy(acc_in, acc_before, sems.at[0])
+        fetch.start()
+    token_ref[...] = jnp.zeros_like(token_ref)
     blocks, listed = list_ref.shape
     low_lanes = lax.broadcasted_iota(jnp.int32, (BLOCK_ROWS, LANES), 1) < HEAD_WIDTH
     low_rows = lax.broadcasted_iota(jnp.int32, (LANES, BLOCK_ROWS), 0) < HEAD_WIDTH
 
     def prepare(block):
         turned[block] = in_ref[block, :BLOCK_ROWS].T[:HEAD_WIDTH]
-        if first:
-            acc_ref[block] = jnp.zeros((BLOCK_ROWS, LANES), jnp.float32)
-        else:
-            acc_ref[block] = acc_before[block]
-            out_ref[block, :HEAD_WIDTH] = gq_before[block]
+        acc_ref[block] = jnp.zeros((BLOCK_ROWS, LANES), jnp.float32)
 
     by_fours(blocks, prepare)
 
@@ -199,17 +198,30 @@
 
     for_tiles(tiles, BACKWARD_TILE, listed, order_ref, count_ref, process)
     if first:
+        store = pltpu.make_async_copy(acc_ref, acc_out, sems.at[0])
+        store.start()
+        store.wait()
         return
+    for i in range(tiles[0] * BACKWARD_TILE):
+        block = order_ref[i]
+        out_ref[block, :HEAD_WIDTH] = gq_before[block]
+    fetch.wait()
     scale = jnp.where(low_lanes, SCORE_SCALE, 1.0)
 
-    def finish(block):
-        out_ref[block, HEAD_WIDTH:] = (acc_ref[block] * scale).astype(jnp.bfloat16)
-
-    by_fours(blocks, finish)
-
-
-def weight_grad_kernel(core_ref, att_ref, up_ref, keep_ref, send_ref):
-    attended = attended_columns(att_ref)
+    def stores(chunk):
+        here = pl.ds(4 * chunk, 4)
+        return pltpu.make_async_copy(out_ref.at[here], out_hbm.at[here], sems.at[1 + chunk])
+
+    for chunk in range(blocks // 4):
+        for block in range(4 * chunk, 4 * chunk + 4):
+            total = acc_ref[block] + acc_before[block]
+            out_ref[block, HEAD_WIDTH:] = (total * scale).astype(jnp.bfloat16)
+        stores(chunk).start()
+    for chunk in range(blocks // 4):
+        stores(chunk).wait()
+
+
+def split_columns_kernel(core_ref, up_ref, keep_ref, send_ref):
     pieces = up_ref.shape[1] // HEAD_WIDTH
 
     def every_other(start):
@@ -220,8 +232,16 @@
 
     even, odd = every_other(0), every_other(1)
     first = core_ref[0] == 0
-    send_ref[...] = dot(attended, jnp.where(first, odd, even), ((1,), (0,))).astype(jnp.bfloat16)
-    keep_ref[...] = dot(attended, jnp.where(first, even, odd), ((1,), (0,)))
+    keep_ref[...] = jnp.where(first, even, odd)
+    send_ref[...] = jnp.where(first, odd, even)
+
+
+def weight_grad_kernel(own_att_ref, other_att_ref, own_up_ref, other_up_ref, token_ref, out_ref):
+    attended = jnp.concatenate(
+        [attended_columns(own_att_ref), attended_columns(other_att_ref)], axis=1
+    )
+    up_rows = jnp.concatenate([own_up_ref[...], other_up_ref[...]], axis=0)
+    out_ref[...] = dot(attended, up_rows, ((1,), (0,))).astype(jnp.bfloat16)
 
 
 def attended_columns(att_ref):
@@ -281,6 +301,18 @@
     smem, vmem = SMEM_SPEC, VMEM_SPEC
 
     packed = exchange(pack(queries[0], keys[0], values[0], up_rows, w_out))
+    half = width // 2
+    core = (lax.axis_index("dp") % 2).reshape(1).astype(jnp.int32)
+    other_core = [(i, i + 1 - 2 * (i % 2)) for i in range(dp_size)]
+    own_up, send_up = call(
+        split_columns_kernel,
+        "split_columns",
+        [shape((local_rows, half), bf16)] * 2,
+        [smem, vmem],
+        flops=10**8,
+    )(core, up_rows)
+    other_up = lax.ppermute(send_up, "dp", other_core)
+    packed, own_up, other_up = lax.optimization_barrier((packed, own_up, other_up))
     packed = packed.reshape(blocks, 2 * BLOCK_ROWS, LANES)
     lists, counts, order = lax.optimization_barrier((lists, counts, by_falling_count(counts)))
     listing = (lists, counts, order)
@@ -298,54 +330,62 @@
     )(*listing, packed)
 
     attended = exchange(attended.reshape(seq_size, near_blocks, HEAD_WIDTH, BLOCK_ROWS))
-    first = call(
+    gq_first, acc_first, token = call(
         functools.partial(backward_kernel, (0, FIRST_TILES), True),
         "backward_first",
-        [half_turned, shape(acc, f32)],
+        [half_turned, shape(acc, f32), shape((8, LANES), f32)],
         [smem] * 3 + [vmem] * 2,
-        [turned],
+        [turned, pltpu.VMEM(acc, f32), pltpu.SemaphoreType.DMA((1,))],
         flops=10 * 10**9,
+        vmem=61,
+        out_specs=[vmem, HBM_SPEC, vmem],
     )(*listing, packed, stats)
 
-    attended, first = lax.optimization_barrier((attended, first))
-    half = width // 2
-    core = (lax.axis_index("dp") % 2).reshape(1).astype(jnp.int32)
-    keep, send = call(
+    attended, token = lax.optimization_barrier((attended, token))
+    (chip_sum,) = call(
         weight_grad_kernel,
         "weight_grad",
-        [shape((width, half), f32), shape((width, half), bf16)],
-        [smem] + [vmem] * 2,
+        [shape((width, half), bf16)],
+        [vmem] * 5,
         flops=10**9,
-    )(core, attended, up_rows)
-    other_core = [(i, i + 1 - 2 * (i % 2)) for i in range(dp_size)]
-    received = lax.ppermute(send, "dp", other_core)
-    chip_sum = (keep + received.astype(f32)).astype(bf16)
-
-    chip_sum, first, attended = lax.optimization_barrier((chip_sum, first, attended))
+    )(attended, lax.ppermute(attended, "dp", other_core), own_up, other_up, token)
+
+    chip_sum, stats = lax.optimization_barrier((chip_sum, stats))
     parts = exchange(chip_sum.reshape(seq_size, width // seq_size, half))
-    (outgoing,) = call(
+    out_shape = (blocks, HEAD_WIDTH + BLOCK_ROWS, LANES)
+    outgoing, token = call(
         functools.partial(backward_kernel, (FIRST_TILES, blocks // BACKWARD_TILE), False),
         "backward_second",
-        [shape((blocks, HEAD_WIDTH + BLOCK_ROWS, LANES), bf16)],
-        [smem] * 3 + [vmem] * 4,
-        [turned, pltpu.VMEM(acc, f32)],
+        [shape(out_shape, bf16), shape((8, LANES), f32)],
+        [smem] * 3 + [vmem] * 3 + [HBM_SPEC],
+        [
+            turned,
+            pltpu.VMEM(acc, f32),
+            pltpu.VMEM(acc, f32),
+            pltpu.VMEM(out_shape, bf16),
+            pltpu.SemaphoreType.DMA((1 + blocks // 4,)),
+        ],
         flops=15 * 10**9,
-    )(*listing, packed, stats, *first)
-
-    parts, outgoing = lax.optimization_barrier((parts, outgoing))
-    seq_sum = jnp.sum(parts.astype(f32), axis=0).astype(bf16)
+        vmem=61,
+        out_specs=[HBM_SPEC, vmem],
+    )(*listing, packed, stats, gq_first, acc_first)
+
+    parts, _ = lax.optimization_barrier((parts, token))
     incoming = exchange(
         outgoing.reshape(seq_size, near_blocks, HEAD_WIDTH + BLOCK_ROWS, LANES)
     )
+    grad_wo = jnp.sum(parts.astype(f32), axis=0)
     chips = dp_size // 2
-    same_core = [[2 * z + c for z in range(chips)] for c in range(2)]
-    seq_sum = jnp.swapaxes(seq_sum.reshape(width // seq_size, chips, half // chips), 0, 1)
-    seq_sum, incoming = lax.optimization_barrier((seq_sum, incoming))
-    terms = lax.all_to_all(
-        seq_sum, "dp", split_axis=0, concat_axis=0, axis_index_groups=same_core, tiled=True
-    )
-    factor = 1.0 / math.sqrt(dp_size * local_rows * seq_size)
-    grad_wo = jnp.sum(terms.astype(f32), axis=0) * factor
+    chip = lax.axis_index("dp") // 2
+    apart = chips // 2
+    while apart:
+        below, above = jnp.split(grad_wo, 2, axis=1)
+        upper = (chip // apart) % 2 == 1
+        opposite = [(i, 2 * ((i // 2) ^ apart) + i % 2) for i in range(dp_size)]
+        received = lax.ppermute(jnp.where(upper, below, above).astype(bf16), "dp", opposite)
+        grad_wo = jnp.where(upper, above, below) + received.astype(f32)
+        apart //= 2
+    grad_wo = grad_wo * (1.0 / math.sqrt(dp_size * local_rows * seq_size))
 
     rows = shape((local_rows, width), bf16)
     (mixed,) = call(mixed_kernel, "mixed", [rows], [vmem] * 2, flops=10**9)(attended, w_out)

time: 152 us -> 133 us (0.88)
  the two profiles are of different devices: /device:TPU:1 before, /device:TPU:192 now
where the time goes in v3:
time: 133 us; the launch traced here: 132 us
  waiting for transfers between devices  51.6 us (39%)
  Pallas kernels  47.7 us (36%)
  starting transfers between devices  28.4 us (21%)
  local copies, waits for them, and re-layouts  2.38 us (2%)
    all_to_all x4, waiting for transfers between devices, exchange(): return lax.all_to_all(array, 'seq', split_axis=0, concat_axis=0, tiled=True)  39.9 us
    all_to_all x4, starting transfers between devices, exchange(): return lax.all_to_all(array, 'seq', split_axis=0, concat_axis=0, tiled=True)  23 us
    pallas_call x1, Pallas kernels, local(): call(functools.partial(backward_kernel, (FIRST_TILES, blocks // BACKWARD_...  16.2 us
    pallas_call x1, Pallas kernels, local(): call(forward_kernel, 'forward', [half_turned, shape((blocks, 8, BLOCK_ROW...  11.9 us
    pallas_call x1, Pallas kernels, local(): call(functools.partial(backward_kernel, (0, FIRST_TILES), True), 'backwar...  10.7 us
    ppermute x3, waiting for transfers between devices, local(): lax.ppermute(jnp.where(upper, below, above).astype(bf16), 'dp', opposite)  8.65 us
    ppermute x3, starting transfers between devices, local(): lax.ppermute(jnp.where(upper, below, above).astype(bf16), 'dp', opposite)  5.3 us
    pallas_call x1, Pallas kernels, pack(): pl.pallas_call(pack_kernel, grid=(steps,), out_shape=jax.ShapeDtypeStruct...  3.92 us
  transfers between devices with their start and end apart: 9, of which 9 were waited for; matrix products, arithmetic and copies ran while one was open for 1% of the time, Pallas kernels for 22%

profile of v3, /device:TPU:192, one launch (start us, length us, event | category | flops | bytes accessed | tf_op | source)
XLA Modules:
  0.0 132.2 jit_solution(17176042556536367416)
XLA Ops:
  0.6 3.9 %pack.1 = bf16[16,2,256,128]{3,2,1,0:T(8,128)(2,1)} custom-call(bf16[256,1024]{1,0:T(8,128)(2,1)} %bitcast.30, bf16[256,1024]{1,0:T(8,128)(2,1)} %bitcast.31, bf16[256,1024]{1,0:T(8,128)(2,1)} %bitcast.32, bf16[256,1024]{1,0:T(8,128)(2,1)} %bitcast.18, bf16[1024,1024]{1,0:T(8,128)(2,1)} %wo_ref.3), custom_call_target="tpu_custom_call" | custom-call | tf_op jit(solution)/shard_map/pack/pallas_call | solution.py:66
  4.6 0.0 copy-start.1
  4.6 0.0 copy-start.4
  4.6 0.0 copy-start.8
  4.6 7.2 %all-to-all-start = ((bf16[16,2,256,128]{3,2,1,0:T(8,128)(2,1)}), bf16[16,2,256,128]{3,2,1,0:T(8,128)(2,1)S(1)}, u32[]{:S(2)}, u32[]{:S(2)}) async-start(bf16[16,2,256,128]{3,2,1,0:T(8,128)(2,1)} %pack.1), calls=%async_computation | async-start | bytes 4194304 | tf_op jit(solution)/shard_map/all_to_all | solution.py:289
  11.8 0.0 copy-done.1
  11.8 0.2 split_columns.1
  12.0 0.1 collective-permute-start
  12.1 0.0 copy-done.4
  12.1 0.0 copy-done.8
  12.1 0.1 copy.13
  12.2 0.0 copy-start.3
  12.2 0.2 convert_reduce_fusion.1
  12.4 0.1 select_reduce_fusion.order_ref
  12.5 0.0 copy-start.5
  12.5 1.1 collective-permute-done.other_up_ref
  13.6 29.8 %all-to-all-done = bf16[16,2,256,128]{3,2,1,0:T(8,128)(2,1)S(1)} async-done(((bf16[16,2,256,128]{3,2,1,0:T(8,128)(2,1)}), bf16[16,2,256,128]{3,2,1,0:T(8,128)(2,1)S(1)}, u32[]{:S(2)}, u32[]{:S(2)}) %all-to-all-start) | async-done | bytes 2097184 | tf_op jit(solution)/shard_map/all_to_all | solution.py:289
  43.4 0.0 copy-start.2
  43.4 11.9 %forward.1 = (bf16[32,64,128]{2,1,0:T(8,128)(2,1)}, f32[32,8,128]{2,1,0:T(8,128)S(1)}) custom-call(s32[32,16]{1,0:T(8,128)S(1)} %bitcast.23, s32[32]{0:T(128)S(1)} %bitcast.28, s32[32]{0:T(128)S(1)} %select_reduce_fusion.order_ref, bf16[32,256,128]{2,1,0:T(8,128)(2,1)S(1)} %bitcast.20), custom_call_target="tpu_custom_call" | custom-call | flops 10000000000 | bytes 4194304 | tf_op jit(solution)/shard_map/forward/pallas_call | solution.py:323
  55.3 0.0 copy-done.3
  55.3 0.0 copy-done.5
  55.3 0.0 copy-done.2
  55.3 0.0 copy-start.7
  55.3 3.8 %all-to-all-start.1 = ((bf16[16,2,64,128]{3,2,1,0:T(8,128)(2,1)}), bf16[16,2,64,128]{3,2,1,0:T(8,128)(2,1)S(1)}, u32[]{:S(2)}, u32[]{:S(2)}) async-start(bf16[16,2,64,128]{3,2,1,0:T(8,128)(2,1)} %bitcast.9), calls=%async_computation.1 | async-start | bytes 1048576 | tf_op jit(solution)/shard_map/all_to_all | solution.py:289
  59.1 0.0 copy-done.7
  59.1 10.7 %backward_first.1 = (bf16[32,64,128]{2,1,0:T(8,128)(2,1)}, f32[32,128,128]{2,1,0:T(8,128)}, f32[8,128]{1,0:T(8,128)}) custom-call(s32[32,16]{1,0:T(8,128)} %bitcast.24, s32[32]{0:T(128)} %bitcast.26, s32[32]{0:T(128)} %copy-done.5, bf16[32,256,128]{2,1,0:T(8,128)(2,1)} %bitcast.21, f32[32,8,128]{2,1,0:T(8,128)} %copy-done.7), custom_call_target="tpu_custom_call" | custom-call | flops 10000000000 | bytes 4194304 | tf_op jit(solution)/shard_map/backward_first/pallas_call | solution.py:333
  69.8 0.6 all-to-all-done.1.att_ref.own_att_ref
  70.4 0.0 collective-permute-start.1
  70.4 1.9 %collective-permute-done.1.other_att_ref = bf16[16,2,64,128]{3,2,1,0:T(8,128)(2,1)S(1)} collective-permute-done((bf16[16,2,64,128]{3,2,1,0:T(8,128)(2,1)S(1)}, bf16[16,2,64,128]{3,2,1,0:T(8,128)(2,1)S(1)}, u32[]{:S(2)}, u32[]{:S(2)}) %collective-permute-start.1) | collective-permute-done | bytes 524320 | tf_op jit(solution)/shard_map/ppermute | solution.py:351
  72.3 0.0 copy-start.6
  72.3 0.7 copy-done.6
  73.0 1.7 %weight_grad.1 = bf16[1024,512]{1,0:T(8,128)(2,1)} custom-call(bf16[16,2,64,128]{3,2,1,0:T(8,128)(2,1)S(1)} %all-to-all-done.1.att_ref.own_att_ref, bf16[16,2,64,128]{3,2,1,0:T(8,128)(2,1)S(1)} %collective-permute-done.1.other_att_ref, bf16[256,512]{1,0:T(8,128)(2,1)S(1)} %get-tuple-element.36.own_up_ref, ...), custom_call_target="tpu_custom_call" | custom-call | flops 1000000000 | bytes 4194304 | tf_op jit(solution)/shard_map/weight_grad/pallas_call | solution.py:345
  74.7 6.5 %all-to-all-start.3 = ((bf16[16,64,512]{2,1,0:T(8,128)(2,1)}), bf16[16,64,512]{2,1,0:T(8,128)(2,1)S(1)}, u32[]{:S(2)}, u32[]{:S(2)}) async-start(bf16[16,64,512]{2,1,0:T(8,128)(2,1)} %bitcast.15), calls=%async_computation.3 | async-start | bytes 2097152 | tf_op jit(solution)/shard_map/all_to_all | solution.py:289
  81.2 16.2 %backward_second.1 = (bf16[32,192,128]{2,1,0:T(8,128)(2,1)}, f32[8,128]{1,0:T(8,128)}) custom-call(s32[32,16]{1,0:T(8,128)} %bitcast.25, s32[32]{0:T(128)} %bitcast.27, s32[32]{0:T(128)} %copy-done.5, bf16[32,256,128]{2,1,0:T(8,128)(2,1)} %bitcast.22, f32[32,8,128]{2,1,0:T(8,128)} %copy-done.7, bf16[32,64,128]{2,1,0:T(8,128)(2,1)} %get-tuple-element.40.refs_0_, ...), custom_call_target="tpu_custom_call" | custom-call | flops 15000000512 | bytes 4194304 | tf_op jit(solution)/shard_map/backward_second/pallas_call | solution.py:356
  97.4 1.6 %all-to-all-done.3 = bf16[16,64,512]{2,1,0:T(8,128)(2,1)S(1)} async-done(((bf16[16,64,512]{2,1,0:T(8,128)(2,1)}), bf16[16,64,512]{2,1,0:T(8,128)(2,1)S(1)}, u32[]{:S(2)}, u32[]{:S(2)}) %all-to-all-start.3) | async-done | bytes 1048608 | tf_op jit(solution)/shard_map/all_to_all | solution.py:289
  99.0 5.6 %all-to-all-start.2 = ((bf16[16,2,192,128]{3,2,1,0:T(8,128)(2,1)}), bf16[16,2,192,128]{3,2,1,0:T(8,128)(2,1)S(1)}, u32[]{:S(2)}, u32[]{:S(2)}) async-start(bf16[16,2,192,128]{3,2,1,0:T(8,128)(2,1)} %bitcast.29), calls=%async_computation.2 | async-start | bytes 3145728 | tf_op jit(solution)/shard_map/all_to_all | solution.py:289
  104.6 0.1 convert_reduce_fusion
  104.8 1.6 %collective-permute-start.2 = (bf16[64,256]{1,0:T(8,128)(2,1)S(1)}, bf16[64,256]{1,0:T(8,128)(2,1)S(1)}, u32[]{:S(2)}, u32[]{:S(2)}) collective-permute-start(bf16[64,256]{1,0:T(8,128)(2,1)S(1)} %select_convert_fusion), channel_id=1, source_target_pairs={{0,128},{16,144},{32,160},{48,176},{64,192},{80,208},{96,224},{112... | collective-permute-start | bytes 98312 | tf_op jit(solution)/shard_map/ppermute | solution.py:385
  106.4 6.3 %collective-permute-done.2 = bf16[64,256]{1,0:T(8,128)(2,1)S(1)} collective-permute-done((bf16[64,256]{1,0:T(8,128)(2,1)S(1)}, bf16[64,256]{1,0:T(8,128)(2,1)S(1)}, u32[]{:S(2)}, u32[]{:S(2)}) %collective-permute-start.2) | collective-permute-done | bytes 32800 | tf_op jit(solution)/shard_map/ppermute | solution.py:385
  112.7 3.7 %collective-permute-start.3 = (bf16[64,128]{1,0:T(8,128)(2,1)S(1)}, bf16[64,128]{1,0:T(8,128)(2,1)S(1)}, u32[]{:S(2)}, u32[]{:S(2)}) collective-permute-start(bf16[64,128]{1,0:T(8,128)(2,1)S(1)} %select_convert_fusion.2), channel_id=1, source_target_pairs={{0,64},{16,80},{32,96},{48,112},{64,0},{80,16},{96,32},{112,48},{1... | collective-permute-start | bytes 49160 | tf_op jit(solution)/shard_map/ppermute | solution.py:385
  116.4 1.7 %collective-permute-done.3 = bf16[64,128]{1,0:T(8,128)(2,1)S(1)} collective-permute-done((bf16[64,128]{1,0:T(8,128)(2,1)S(1)}, bf16[64,128]{1,0:T(8,128)(2,1)S(1)}, u32[]{:S(2)}, u32[]{:S(2)}) %collective-permute-start.3) | collective-permute-done | bytes 16416 | tf_op jit(solution)/shard_map/ppermute | solution.py:385
  118.2 0.1 select_convert_fusion.1
  118.3 0.0 collective-permute-start.4
  118.3 0.0 copy-start
  118.3 1.6 %copy-done = bf16[1024,1024]{1,0:T(8,128)(2,1)S(1)} copy-done((bf16[1024,1024]{1,0:T(8,128)(2,1)S(1)}, bf16[1024,1024]{1,0:T(8,128)(2,1)}, u32[]{:S(2)}) %copy-start) | copy-done | bytes 2097176
  119.9 1.5 %mixed.1 = bf16[256,1024]{1,0:T(8,128)(2,1)} custom-call(bf16[16,2,64,128]{3,2,1,0:T(8,128)(2,1)S(1)} %all-to-all-done.1.att_ref.own_att_ref, bf16[1024,1024]{1,0:T(8,128)(2,1)S(1)} %copy-done), custom_call_target="tpu_custom_call" | custom-call | flops 1000000000 | bytes 4194304 | tf_op jit(solution)/shard_map/mixed/pallas_call | solution.py:391
  121.4 0.6 collective-permute-done.4
  122.0 0.7 add_multiply_fusion
  122.7 7.9 %all-to-all-done.2.in_ref = bf16[16,2,192,128]{3,2,1,0:T(8,128)(2,1)S(1)} async-done(((bf16[16,2,192,128]{3,2,1,0:T(8,128)(2,1)}), bf16[16,2,192,128]{3,2,1,0:T(8,128)(2,1)S(1)}, u32[]{:S(2)}, u32[]{:S(2)}) %all-to-all-start.2) | async-done | bytes 1572896 | tf_op jit(solution)/shard_map/all_to_all | solution.py:289
  130.6 1.6 %unpack.1 = (bf16[256,1024]{1,0:T(8,128)(2,1)}, bf16[256,1024]{1,0:T(8,128)(2,1)}, bf16[256,1024]{1,0:T(8,128)(2,1)}) custom-call(bf16[16,2,192,128]{3,2,1,0:T(8,128)(2,1)S(1)} %all-to-all-done.2.in_ref), custom_call_target="tpu_custom_call" | custom-call | bytes 4194304 | tf_op jit(solution)/shard_map/unpack/pallas_call | solution.py:392
  (6 shorter events, 0.0 us)
Async XLA Ops:
  4.6 7.2 %copy-start.1 = (bf16[1,256,1024]{2,1,0:T(8,128)(2,1)S(1)}, bf16[1,256,1024]{2,1,0:T(8,128)(2,1)}, u32[]{:S(2)}) copy-start(bf16[1,256,1024]{2,1,0:T(8,128)(2,1)} %param.10) | copy-start | bytes 1572868
  4.6 7.5 %copy-start.4 = (s32[1,32]{1,0:T(1,128)S(1)}, s32[1,32]{1,0:T(1,128)}, u32[]{:S(2)}) copy-start(s32[1,32]{1,0:T(1,128)} %param.13) | copy-start | bytes 388
  4.6 7.6 %copy-start.8 = (s32[1,32,16]{1,2,0:T(8,128)S(1)}, s32[1,32,16]{1,2,0:T(8,128)}, u32[]{:S(2)}) copy-start(s32[1,32,16]{1,2,0:T(8,128)} %param.12) | copy-start | bytes 6148
  4.6 38.8 %all-to-all-start = ((bf16[16,2,256,128]{3,2,1,0:T(8,128)(2,1)}), bf16[16,2,256,128]{3,2,1,0:T(8,128)(2,1)S(1)}, u32[]{:S(2)}, u32[]{:S(2)}) async-start(bf16[16,2,256,128]{3,2,1,0:T(8,128)(2,1)} %pack.1), calls=%async_computation | async-start | bytes 4194304 | tf_op jit(solution)/shard_map/all_to_all | solution.py:289
  12.0 1.6 %collective-permute-start = (bf16[256,512]{1,0:T(8,128)(2,1)S(1)}, bf16[256,512]{1,0:T(8,128)(2,1)S(1)}, u32[]{:S(2)}, u32[]{:S(2)}) collective-permute-start(bf16[256,512]{1,0:T(8,128)(2,1)S(1)} %get-tuple-element.30), channel_id=1, source_target_pairs={{0,16},{16,0},{32,48},{48,32},{64,80},{80,64},{96,112},{112,96},{1... | collective-permute-start | bytes 786440 | tf_op jit(solution)/shard_map/ppermute | solution.py:314
  12.2 43.1 %copy-start.3 = (s32[1,32,16]{2,1,0:T(8,128)}, s32[1,32,16]{2,1,0:T(8,128)S(1)}, u32[]{:S(2)}) copy-start(s32[1,32,16]{2,1,0:T(8,128)S(1)} %copy.13) | copy-start | bytes 6148
  12.5 42.8 %copy-start.5 = (s32[32]{0:T(128)}, s32[32]{0:T(128)S(1)}, u32[]{:S(2)}) copy-start(s32[32]{0:T(128)S(1)} %select_reduce_fusion.order_ref) | copy-start | bytes 388
  43.4 11.9 %copy-start.2 = (bf16[16,2,256,128]{3,2,1,0:T(8,128)(2,1)}, bf16[16,2,256,128]{3,2,1,0:T(8,128)(2,1)S(1)}, u32[]{:S(2)}) copy-start(bf16[16,2,256,128]{3,2,1,0:T(8,128)(2,1)S(1)} %all-to-all-done) | copy-start | bytes 6291460
  55.3 3.8 %copy-start.7 = (f32[32,8,128]{2,1,0:T(8,128)}, f32[32,8,128]{2,1,0:T(8,128)S(1)}, u32[]{:S(2)}) copy-start(f32[32,8,128]{2,1,0:T(8,128)S(1)} %get-tuple-element.39.stat_ref) | copy-start | bytes 393220
  55.3 15.1 %all-to-all-start.1 = ((bf16[16,2,64,128]{3,2,1,0:T(8,128)(2,1)}), bf16[16,2,64,128]{3,2,1,0:T(8,128)(2,1)S(1)}, u32[]{:S(2)}, u32[]{:S(2)}) async-start(bf16[16,2,64,128]{3,2,1,0:T(8,128)(2,1)} %bitcast.9), calls=%async_computation.1 | async-start | bytes 1048576 | tf_op jit(solution)/shard_map/all_to_all | solution.py:289
  70.4 1.9 %collective-permute-start.1 = (bf16[16,2,64,128]{3,2,1,0:T(8,128)(2,1)S(1)}, bf16[16,2,64,128]{3,2,1,0:T(8,128)(2,1)S(1)}, u32[]{:S(2)}, u32[]{:S(2)}) collective-permute-start(bf16[16,2,64,128]{3,2,1,0:T(8,128)(2,1)S(1)} %all-to-all-done.1.att_ref.own_att_ref), channel_id=1, source_target_pairs={{0,16},{16,0},{32,48},{48,32},{64,80},{80,64},{96,112},{112,96},{1... | collective-permute-start | bytes 1572872 | tf_op jit(solution)/shard_map/ppermute | solution.py:351
  72.3 0.7 copy-start.6
  74.7 24.3 %all-to-all-start.3 = ((bf16[16,64,512]{2,1,0:T(8,128)(2,1)}), bf16[16,64,512]{2,1,0:T(8,128)(2,1)S(1)}, u32[]{:S(2)}, u32[]{:S(2)}) async-start(bf16[16,64,512]{2,1,0:T(8,128)(2,1)} %bitcast.15), calls=%async_computation.3 | async-start | bytes 2097152 | tf_op jit(solution)/shard_map/all_to_all | solution.py:289
  99.0 31.6 %all-to-all-start.2 = ((bf16[16,2,192,128]{3,2,1,0:T(8,128)(2,1)}), bf16[16,2,192,128]{3,2,1,0:T(8,128)(2,1)S(1)}, u32[]{:S(2)}, u32[]{:S(2)}) async-start(bf16[16,2,192,128]{3,2,1,0:T(8,128)(2,1)} %bitcast.29), calls=%async_computation.2 | async-start | bytes 3145728 | tf_op jit(solution)/shard_map/all_to_all | solution.py:289
  104.8 7.9 %collective-permute-start.2 = (bf16[64,256]{1,0:T(8,128)(2,1)S(1)}, bf16[64,256]{1,0:T(8,128)(2,1)S(1)}, u32[]{:S(2)}, u32[]{:S(2)}) collective-permute-start(bf16[64,256]{1,0:T(8,128)(2,1)S(1)} %select_convert_fusion), channel_id=1, source_target_pairs={{0,128},{16,144},{32,160},{48,176},{64,192},{80,208},{96,224},{112... | collective-permute-start | bytes 98312 | tf_op jit(solution)/shard_map/ppermute | solution.py:385
  112.7 5.4 %collective-permute-start.3 = (bf16[64,128]{1,0:T(8,128)(2,1)S(1)}, bf16[64,128]{1,0:T(8,128)(2,1)S(1)}, u32[]{:S(2)}, u32[]{:S(2)}) collective-permute-start(bf16[64,128]{1,0:T(8,128)(2,1)S(1)} %select_convert_fusion.2), channel_id=1, source_target_pairs={{0,64},{16,80},{32,96},{48,112},{64,0},{80,16},{96,32},{112,48},{1... | collective-permute-start | bytes 49160 | tf_op jit(solution)/shard_map/ppermute | solution.py:385
  118.3 3.8 %collective-permute-start.4 = (bf16[64,64]{1,0:T(8,128)(2,1)S(1)}, bf16[64,64]{1,0:T(8,128)(2,1)S(1)}, u32[]{:S(2)}, u32[]{:S(2)}) collective-permute-start(bf16[64,64]{1,0:T(8,128)(2,1)S(1)} %select_convert_fusion.1), channel_id=1, source_target_pairs={{0,32},{16,48},{32,0},{48,16},{64,96},{80,112},{96,64},{112,80},{1... | collective-permute-start | bytes 24584 | tf_op jit(solution)/shard_map/ppermute | solution.py:385
  118.3 1.6 %copy-start = (bf16[1024,1024]{1,0:T(8,128)(2,1)S(1)}, bf16[1024,1024]{1,0:T(8,128)(2,1)}, u32[]{:S(2)}) copy-start(bf16[1024,1024]{1,0:T(8,128)(2,1)} %wo_ref.3) | copy-start | bytes 6291460

commit v4 on v3

--- a/solution.py
+++ b/solution.py
@@ -44,7 +44,40 @@
     )
 
 
-def pack_kernel(query_ref, key_ref, value_ref, up_ref, wo_ref, out_ref):
+def sort_by_falling_count(count_ref, order_ref, place_ref):
+    places = place_ref.shape[0]
+    for i in range(places):
+        place_ref[i] = 0
+
+    def tally(block, _):
+        count = count_ref[block]
+        place_ref[count] = place_ref[count] + 1
+        return 0
+
+    lax.fori_loop(0, count_ref.shape[0], tally, 0)
+    before = jnp.int32(0)
+    for i in reversed(range(places)):
+        here = place_ref[i]
+        place_ref[i] = before
+        before = before + here
+
+    def put(block, _):
+        count = count_ref[block]
+        place = place_ref[count]
+        order_ref[place] = block
+        place_ref[count] = place + 1
+        return 0
+
+    lax.fori_loop(0, count_ref.shape[0], put, 0)
+
+
+def pack_kernel(
+    count_ref, query_ref, key_ref, value_ref, up_ref, wo_ref, out_ref, order_ref, place_ref
+):
+    @pl.when(pl.program_id(0) == 0)
+    def _():
+        sort_by_falling_count(count_ref, order_ref, place_ref)
+
     grads = dot(up_ref[...], wo_ref[...], ((1,), (1,))).astype(jnp.bfloat16)
     heads_here = out_ref.shape[0]
     for head in range(heads_here):
@@ -57,7 +90,7 @@
             out_ref[head, block, BLOCK_ROWS:] = qg[rows]
 
 
-def pack(queries, keys, values, up_rows, w_out):
+def pack(counts, listed, queries, keys, values, up_rows, w_out):
     rows, width = queries.shape
     blocks = rows // BLOCK_ROWS
     steps = 2
@@ -66,20 +99,26 @@
     return pl.pallas_call(
         pack_kernel,
         grid=(steps,),
-        out_shape=jax.ShapeDtypeStruct((HEADS, blocks, 2 * BLOCK_ROWS, LANES), jnp.bfloat16),
+        out_shape=[
+            jax.ShapeDtypeStruct((HEADS, blocks, 2 * BLOCK_ROWS, LANES), jnp.bfloat16),
+            jax.ShapeDtypeStruct(counts.shape, jnp.int32),
+        ],
         in_specs=[
+            SMEM_SPEC,
             part,
             part,
             part,
             pl.BlockSpec((rows, width), lambda i: (0, 0)),
             pl.BlockSpec((columns, width), lambda i: (i, 0)),
         ],
-        out_specs=pl.BlockSpec(
-            (HEADS // steps, blocks, 2 * BLOCK_ROWS, LANES), lambda i: (i, 0, 0, 0)
-        ),
+        out_specs=[
+            pl.BlockSpec((HEADS // steps, blocks, 2 * BLOCK_ROWS, LANES), lambda i: (i, 0, 0, 0)),
+            SMEM_SPEC,
+        ],
+        scratch_shapes=[pltpu.SMEM((listed + 1,), jnp.int32)],
         compiler_params=pltpu.CompilerParams(vmem_limit_bytes=60 * 2**20),
         name="pack",
-    )(queries, keys, values, up_rows, w_out)
+    )(counts, queries, keys, values, up_rows, w_out)
 
 
 def for_tiles(tiles, tile_blocks, listed, order_ref, count_ref, process):
@@ -103,7 +142,7 @@
 
 
 def forward_kernel(list_ref, count_ref, order_ref, in_ref, att_ref, stat_ref, turned, *score_bufs):
-    blocks, listed = list_ref.shape
+    listed, blocks = list_ref.shape
     low = lax.broadcasted_iota(jnp.int32, (LANES, BLOCK_ROWS), 0) < HEAD_WIDTH
 
     def turn(block):
@@ -114,7 +153,7 @@
     def process(members, slots):
         qg_turned = [in_ref[block, BLOCK_ROWS:].T for block in members]
         queries = [jnp.where(low, array, jnp.zeros_like(array)) for array in qg_turned]
-        near = [[list_ref[block, slot] for slot in range(slots)] for block in members]
+        near = [[list_ref[slot, block] for slot in range(slots)] for block in members]
         highest = []
         for i, block in enumerate(members):
             rows = jnp.concatenate([in_ref[key, :BLOCK_ROWS] for key in near[i]], axis=0)
@@ -146,13 +185,13 @@
 
 def backward_kernel(tiles, first, list_ref, count_ref, order_ref, in_ref, stat_ref, *refs):
     if first:
-        out_ref, acc_out, token_ref, turned, acc_ref, sems = refs
+        out_ref, token_ref, turned, acc_ref = refs
     else:
-        gq_before, acc_in, out_hbm, token_ref, turned, acc_ref, acc_before, out_ref, sems = refs
-        fetch = pltpu.make_async_copy(acc_in, acc_before, sems.at[0])
+        part_hbm, out_hbm, token_ref, turned, acc_ref, out_ref, sems = refs
+        fetch = pltpu.make_async_copy(part_hbm, out_ref, sems.at[0])
         fetch.start()
     token_ref[...] = jnp.zeros_like(token_ref)
-    blocks, listed = list_ref.shape
+    listed, blocks = list_ref.shape
     low_lanes = lax.broadcasted_iota(jnp.int32, (BLOCK_ROWS, LANES), 1) < HEAD_WIDTH
     low_rows = lax.broadcasted_iota(jnp.int32, (LANES, BLOCK_ROWS), 0) < HEAD_WIDTH
 
@@ -161,6 +200,8 @@
         acc_ref[block] = jnp.zeros((BLOCK_ROWS, LANES), jnp.float32)
 
     by_fours(blocks, prepare)
+    if not first:
+        fetch.wait()
 
     def process(members, slots):
         for block in members:
@@ -174,7 +215,7 @@
                 [jnp.where(low_lanes, qg, zero), jnp.where(low_lanes, zero, qg)], axis=0
             )
             top, delta = stat_ref[block, 0:1], stat_ref[block, 1:2]
-            near = [list_ref[block, slot] for slot in range(slots)]
+            near = [list_ref[slot, block] for slot in range(slots)]
             rows = jnp.concatenate([in_ref[key, :BLOCK_ROWS] for key in near], axis=0)
             both = dot(rows, across, ((1,), (0,)))
             joined = []
@@ -198,14 +239,12 @@
 
     for_tiles(tiles, BACKWARD_TILE, listed, order_ref, count_ref, process)
     if first:
-        store = pltpu.make_async_copy(acc_ref, acc_out, sems.at[0])
-        store.start()
-        store.wait()
+
+        def keep(block):
+            out_ref[block, HEAD_WIDTH:] = acc_ref[block].astype(jnp.bfloat16)
+
+        by_fours(blocks, keep)
         return
-    for i in range(tiles[0] * BACKWARD_TILE):
-        block = order_ref[i]
-        out_ref[block, :HEAD_WIDTH] = gq_before[block]
-    fetch.wait()
     scale = jnp.where(low_lanes, SCORE_SCALE, 1.0)
 
     def stores(chunk):
@@ -214,7 +253,7 @@
 
     for chunk in range(blocks // 4):
         for block in range(4 * chunk, 4 * chunk + 4):
-            total = acc_ref[block] + acc_before[block]
+            total = acc_ref[block] + out_ref[block, HEAD_WIDTH:].astype(jnp.float32)
             out_ref[block, HEAD_WIDTH:] = (total * scale).astype(jnp.bfloat16)
         stores(chunk).start()
     for chunk in range(blocks // 4):
@@ -278,13 +317,6 @@
             )
 
 
-def by_falling_count(counts):
-    index = jnp.arange(counts.shape[0], dtype=jnp.int32)
-    place = -counts * counts.shape[0] + index
-    rank = jnp.sum((place[None, :] < place[:, None]).astype(jnp.int32), axis=1)
-    return jnp.sum(jnp.where(rank[None, :] == index[:, None], index[None, :], 0), axis=1)
-
-
 def exchange(array):
     return lax.all_to_all(array, "seq", split_axis=0, concat_axis=0, tiled=True)
 
@@ -292,15 +324,17 @@
 def local(queries, keys, values, upstream, w_out, key_blocks, block_counts):
     local_rows, width = queries.shape[1:]
     seq_size, dp_size = lax.axis_size("seq"), lax.axis_size("dp")
-    lists, counts = key_blocks[0], block_counts[0]
-    blocks, listed = lists.shape
+    lists, counts = key_blocks[0].T, block_counts[0]
+    listed, blocks = lists.shape
     near_blocks = local_rows // BLOCK_ROWS
     up_rows = upstream[0]
     bf16, f32 = jnp.bfloat16, jnp.float32
     shape = jax.ShapeDtypeStruct
     smem, vmem = SMEM_SPEC, VMEM_SPEC
 
-    packed = exchange(pack(queries[0], keys[0], values[0], up_rows, w_out))
+    packed, order = pack(counts, listed, queries[0], keys[0], values[0], up_rows, w_out)
+    packed = exchange(packed)
+    packed, up_rows = lax.optimization_barrier((packed, up_rows))
     half = width // 2
     core = (lax.axis_index("dp") % 2).reshape(1).astype(jnp.int32)
     other_core = [(i, i + 1 - 2 * (i % 2)) for i in range(dp_size)]
@@ -312,9 +346,7 @@
         flops=10**8,
     )(core, up_rows)
     other_up = lax.ppermute(send_up, "dp", other_core)
-    packed, own_up, other_up = lax.optimization_barrier((packed, own_up, other_up))
     packed = packed.reshape(blocks, 2 * BLOCK_ROWS, LANES)
-    lists, counts, order = lax.optimization_barrier((lists, counts, by_falling_count(counts)))
     listing = (lists, counts, order)
     turned = pltpu.VMEM((blocks, HEAD_WIDTH, BLOCK_ROWS), bf16)
     acc = (blocks, BLOCK_ROWS, LANES)
@@ -330,15 +362,14 @@
     )(*listing, packed)
 
     attended = exchange(attended.reshape(seq_size, near_blocks, HEAD_WIDTH, BLOCK_ROWS))
-    gq_first, acc_first, token = call(
+    out_shape = (blocks, HEAD_WIDTH + BLOCK_ROWS, LANES)
+    outgoing, token = call(
         functools.partial(backward_kernel, (0, FIRST_TILES), True),
         "backward_first",
-        [half_turned, shape(acc, f32), shape((8, LANES), f32)],
+        [shape(out_shape, bf16), shape((8, LANES), f32)],
         [smem] * 3 + [vmem] * 2,
-        [turned, pltpu.VMEM(acc, f32), pltpu.SemaphoreType.DMA((1,))],
+        [turned, pltpu.VMEM(acc, f32)],
         flops=10 * 10**9,
-        vmem=61,
-        out_specs=[vmem, HBM_SPEC, vmem],
     )(*listing, packed, stats)
 
     attended, token = lax.optimization_barrier((attended, token))
@@ -352,15 +383,13 @@
 
     chip_sum, stats = lax.optimization_barrier((chip_sum, stats))
     parts = exchange(chip_sum.reshape(seq_size, width // seq_size, half))
-    out_shape = (blocks, HEAD_WIDTH + BLOCK_ROWS, LANES)
     outgoing, token = call(
         functools.partial(backward_kernel, (FIRST_TILES, blocks // BACKWARD_TILE), False),
         "backward_second",
         [shape(out_shape, bf16), shape((8, LANES), f32)],
-        [smem] * 3 + [vmem] * 3 + [HBM_SPEC],
+        [smem] * 3 + [vmem] * 2 + [HBM_SPEC],
         [
             turned,
-            pltpu.VMEM(acc, f32),
             pltpu.VMEM(acc, f32),
             pltpu.VMEM(out_shape, bf16),
             pltpu.SemaphoreType.DMA((1 + blocks // 4,)),
@@ -368,7 +397,7 @@
         flops=15 * 10**9,
         vmem=61,
         out_specs=[HBM_SPEC, vmem],
-    )(*listing, packed, stats, gq_first, acc_first)
+    )(*listing, packed, stats, outgoing)
 
     parts, _ = lax.optimization_barrier((parts, token))
     incoming = exchange(

time: 133 us -> 129 us (0.970)
  blocking collectives: 0 us -> 35.6 us
  waiting for transfers between devices: 51.6 us -> 20.1 us
  starting transfers between devices: 28.4 us -> 21.3 us
    all_to_all x0 -> x1, blocking collectives: none -> 35.6 us  [exchange(): return lax.all_to_all(array, 'seq', split_axis=0, concat_axis=0, tiled=True)]
    all_to_all x4 -> x3, waiting for transfers between devices: 39.9 us -> 8.55 us  [exchange(): return lax.all_to_all(array, 'seq', split_axis=0, concat_axis=0, tiled=True)]
    all_to_all x4 -> x3, starting transfers between devices: 23 us -> 16.2 us  [exchange(): return lax.all_to_all(array, 'seq', split_axis=0, concat_axis=0, tiled=True)]
    pallas_call x1, Pallas kernels: 10.7 us -> 8.02 us  [local(): call(functools.partial(backward_kernel, (0, FIRST_TILES), True), 'backwar...]
    ppermute x1, waiting for transfers between devices: 1.91 us -> 0.01 us  [local(): lax.ppermute(attended, 'dp', other_core)]
    ppermute x3, waiting for transfers between devices: 8.65 us -> 10 us  [local(): lax.ppermute(jnp.where(upper, below, above).astype(bf16), 'dp', opposite)]
    unnamed x19 -> x16, local copies, waits for them, and re-layouts: 2.38 us -> 2.76 us
  transfers between devices with their start and end apart: 9 -> 8, of which waited for: 9 -> 6; matrix products, arithmetic and copies ran while one was open for 1% -> 1% of each run, Pallas kernels for 22% -> 21%
where the time goes in v4:
time: 129 us
  Pallas kernels  47.5 us (37%)
  blocking collectives  35.6 us (28%)
  starting transfers between devices  21.3 us (17%)
  waiting for transfers between devices  20.1 us (16%)
  local copies, waits for them, and re-layouts  2.76 us (2%)
    all_to_all x1, blocking collectives, exchange(): return lax.all_to_all(array, 'seq', split_axis=0, concat_axis=0, tiled=True)  35.6 us
    pallas_call x1, Pallas kernels, local(): call(functools.partial(backward_kernel, (FIRST_TILES, blocks // BACKWARD_...  17.3 us
    all_to_all x3, starting transfers between devices, exchange(): return lax.all_to_all(array, 'seq', split_axis=0, concat_axis=0, tiled=True)  16.2 us
    pallas_call x1, Pallas kernels, local(): call(forward_kernel, 'forward', [half_turned, shape((blocks, 8, BLOCK_ROW...  12.5 us
    ppermute x3, waiting for transfers between devices, local(): lax.ppermute(jnp.where(upper, below, above).astype(bf16), 'dp', opposite)  10 us
    all_to_all x3, waiting for transfers between devices, exchange(): return lax.all_to_all(array, 'seq', split_axis=0, concat_axis=0, tiled=True)  8.55 us
    pallas_call x1, Pallas kernels, local(): call(functools.partial(backward_kernel, (0, FIRST_TILES), True), 'backwar...  8.02 us
    pallas_call x1, Pallas kernels, pack(): pl.pallas_call(pack_kernel, grid=(steps,), out_shape=[jax.ShapeDtypeStruc...  4.59 us
  transfers between devices with their start and end apart: 8, of which 6 were waited for; matrix products, arithmetic and copies ran while one was open for 1% of the time, Pallas kernels for 21%

profile of v4, /device:TPU:192, one launch (start us, length us, event | category | flops | bytes accessed | tf_op | source)
XLA Modules:
  0.0 128.9 jit_solution(15916659283607598786)
XLA Ops:
  0.6 4.6 %pack.1 = (bf16[16,2,256,128]{3,2,1,0:T(8,128)(2,1)}, s32[32]{0:T(128)}) custom-call(s32[32]{0:T(128)} %bitcast.22, bf16[256,1024]{1,0:T(8,128)(2,1)} %bitcast.30, bf16[256,1024]{1,0:T(8,128)(2,1)} %bitcast.31, bf16[256,1024]{1,0:T(8,128)(2,1)} %bitcast.32, bf16[256,1024]{1,0:T(8,128)(2,1)} %bitcast.17, bf16[1024,1024]{1,0:T(8,128)(2,1)} %wo_ref.3), custom_call_target="tpu_custom_call" | custom-call | tf_op jit(solution)/shard_map/pack/pallas_call | solution.py:99
  5.2 0.0 copy-start.3
  5.2 0.0 copy-start.4
  5.2 0.0 copy-start.5
  5.2 35.6 %all_to_all.20 = bf16[16,2,256,128]{3,2,1,0:T(8,128)(2,1)S(1)} all-to-all(bf16[16,2,256,128]{3,2,1,0:T(8,128)(2,1)} %get-tuple-element.24), channel_id=1, replica_groups=mesh['dp'=16,'seq'=16] {'seq'}, dimensions={0} | all-to-all | bytes 4194304 | tf_op jit(solution)/shard_map/all_to_all | solution.py:321
  40.8 0.0 copy-start.2
  40.8 0.0 copy-done.3
  40.8 0.0 copy-done.4
  40.8 0.0 copy-done.5
  40.8 12.5 %forward.1 = (bf16[32,64,128]{2,1,0:T(8,128)(2,1)}, f32[32,8,128]{2,1,0:T(8,128)S(1)}) custom-call(s32[16,32]{1,0:T(8,128)S(1)} %bitcast.27, s32[32]{0:T(128)S(1)} %bitcast.24, s32[32]{0:T(128)S(1)} %copy-done.5, bf16[32,256,128]{2,1,0:T(8,128)(2,1)S(1)} %bitcast.19), custom_call_target="tpu_custom_call" | custom-call | flops 10000000000 | bytes 4194304 | tf_op jit(solution)/shard_map/forward/pallas_call | solution.py:355
  53.4 0.0 copy-start.7
  53.4 3.8 %all-to-all-start.1 = ((bf16[16,2,64,128]{3,2,1,0:T(8,128)(2,1)}), bf16[16,2,64,128]{3,2,1,0:T(8,128)(2,1)S(1)}, u32[]{:S(2)}, u32[]{:S(2)}) async-start(bf16[16,2,64,128]{3,2,1,0:T(8,128)(2,1)} %bitcast.8), calls=%async_computation.1 | async-start | bytes 1048576 | tf_op jit(solution)/shard_map/all_to_all | solution.py:321
  57.1 0.0 copy-done.2
  57.1 0.0 copy-start
  57.2 8.0 %backward_first.1 = (bf16[32,192,128]{2,1,0:T(8,128)(2,1)S(1)}, f32[8,128]{1,0:T(8,128)S(1)}) custom-call(s32[16,32]{1,0:T(8,128)S(1)} %bitcast.28, s32[32]{0:T(128)S(1)} %bitcast.25, s32[32]{0:T(128)S(1)} %copy-done.5, bf16[32,256,128]{2,1,0:T(8,128)(2,1)S(1)} %bitcast.20, f32[32,8,128]{2,1,0:T(8,128)S(1)} %get-tuple-element.34.stat_ref), custom_call_target="tpu_custom_call" | custom-call | flops 10000000000 | bytes 4194304 | tf_op jit(solution)/shard_map/backward_first/pallas_call | solution.py:366
  65.2 0.0 copy-done.7
  65.2 0.0 copy-start.6
  65.2 1.1 copy-done.6
  66.3 1.3 %all-to-all-done.1.att_ref.own_att_ref = bf16[16,2,64,128]{3,2,1,0:T(8,128)(2,1)S(1)} async-done(((bf16[16,2,64,128]{3,2,1,0:T(8,128)(2,1)}), bf16[16,2,64,128]{3,2,1,0:T(8,128)(2,1)S(1)}, u32[]{:S(2)}, u32[]{:S(2)}) %all-to-all-start.1) | async-done | bytes 524320 | tf_op jit(solution)/shard_map/all_to_all | solution.py:321
  67.6 0.0 collective-permute-start
  67.6 0.0 copy-done
  67.6 0.2 split_columns.1
  67.9 0.6 collective-permute-start.1
  68.5 1.5 %collective-permute-done.1.other_up_ref = bf16[256,512]{1,0:T(8,128)(2,1)S(1)} collective-permute-done((bf16[256,512]{1,0:T(8,128)(2,1)S(1)}, bf16[256,512]{1,0:T(8,128)(2,1)S(1)}, u32[]{:S(2)}, u32[]{:S(2)}) %collective-permute-start.1) | collective-permute-done | bytes 262176 | tf_op jit(solution)/shard_map/ppermute | solution.py:348
  69.9 0.0 collective-permute-done.other_att_ref
  69.9 1.7 %weight_grad.1 = bf16[1024,512]{1,0:T(8,128)(2,1)} custom-call(bf16[16,2,64,128]{3,2,1,0:T(8,128)(2,1)S(1)} %all-to-all-done.1.att_ref.own_att_ref, bf16[16,2,64,128]{3,2,1,0:T(8,128)(2,1)S(1)} %collective-permute-done.other_att_ref, bf16[256,512]{1,0:T(8,128)(2,1)S(1)} %get-tuple-element.31.own_up_ref, ...), custom_call_target="tpu_custom_call" | custom-call | flops 1000000000 | bytes 4194304 | tf_op jit(solution)/shard_map/weight_grad/pallas_call | solution.py:376
  71.6 5.7 %all-to-all-start.3 = ((bf16[16,64,512]{2,1,0:T(8,128)(2,1)}), bf16[16,64,512]{2,1,0:T(8,128)(2,1)S(1)}, u32[]{:S(2)}, u32[]{:S(2)}) async-start(bf16[16,64,512]{2,1,0:T(8,128)(2,1)} %bitcast.16), calls=%async_computation.3 | async-start | bytes 2097152 | tf_op jit(solution)/shard_map/all_to_all | solution.py:321
  77.3 17.3 %backward_second.1 = (bf16[32,192,128]{2,1,0:T(8,128)(2,1)}, f32[8,128]{1,0:T(8,128)}) custom-call(s32[16,32]{1,0:T(8,128)} %bitcast.26, s32[32]{0:T(128)} %bitcast.23, s32[32]{0:T(128)} %get-tuple-element.23.order_ref, bf16[32,256,128]{2,1,0:T(8,128)(2,1)} %bitcast.21, f32[32,8,128]{2,1,0:T(8,128)} %copy-done.7, bf16[32,192,128]{2,1,0:T(8,128)(2,1)} %copy-done.6), custom_call_target="tpu_custom_call" | custom-call | flops 15000000512 | bytes 4194304 | tf_op jit(solution)/shard_map/backward_second/pallas_call | solution.py:386
  94.7 0.5 all-to-all-done.3
  95.1 6.8 %all-to-all-start.2 = ((bf16[16,2,192,128]{3,2,1,0:T(8,128)(2,1)}), bf16[16,2,192,128]{3,2,1,0:T(8,128)(2,1)S(1)}, u32[]{:S(2)}, u32[]{:S(2)}) async-start(bf16[16,2,192,128]{3,2,1,0:T(8,128)(2,1)} %bitcast.29), calls=%async_computation.2 | async-start | bytes 3145728 | tf_op jit(solution)/shard_map/all_to_all | solution.py:321
  101.9 0.1 convert_reduce_fusion
  102.1 0.1 collective-permute-start.2
  102.2 7.8 %collective-permute-done.2 = bf16[64,256]{1,0:T(8,128)(2,1)S(1)} collective-permute-done((bf16[64,256]{1,0:T(8,128)(2,1)S(1)}, bf16[64,256]{1,0:T(8,128)(2,1)S(1)}, u32[]{:S(2)}, u32[]{:S(2)}) %collective-permute-start.2) | collective-permute-done | bytes 32800 | tf_op jit(solution)/shard_map/ppermute | solution.py:414
  110.0 2.5 %collective-permute-start.3 = (bf16[64,128]{1,0:T(8,128)(2,1)S(1)}, bf16[64,128]{1,0:T(8,128)(2,1)S(1)}, u32[]{:S(2)}, u32[]{:S(2)}) collective-permute-start(bf16[64,128]{1,0:T(8,128)(2,1)S(1)} %select_convert_fusion.2), channel_id=1, source_target_pairs={{0,64},{16,80},{32,96},{48,112},{64,0},{80,16},{96,32},{112,48},{1... | collective-permute-start | bytes 49160 | tf_op jit(solution)/shard_map/ppermute | solution.py:414
  112.5 2.3 %collective-permute-done.3 = bf16[64,128]{1,0:T(8,128)(2,1)S(1)} collective-permute-done((bf16[64,128]{1,0:T(8,128)(2,1)S(1)}, bf16[64,128]{1,0:T(8,128)(2,1)S(1)}, u32[]{:S(2)}, u32[]{:S(2)}) %collective-permute-start.3) | collective-permute-done | bytes 16416 | tf_op jit(solution)/shard_map/ppermute | solution.py:414
  114.7 0.1 select_convert_fusion.1
  114.8 1.9 %collective-permute-start.4 = (bf16[64,64]{1,0:T(8,128)(2,1)S(1)}, bf16[64,64]{1,0:T(8,128)(2,1)S(1)}, u32[]{:S(2)}, u32[]{:S(2)}) collective-permute-start(bf16[64,64]{1,0:T(8,128)(2,1)S(1)} %select_convert_fusion.1), channel_id=1, source_target_pairs={{0,32},{16,48},{32,0},{48,16},{64,96},{80,112},{96,64},{112,80},{1... | collective-permute-start | bytes 24584 | tf_op jit(solution)/shard_map/ppermute | solution.py:414
  116.7 0.0 copy-start.1
  116.7 1.6 %copy-done.1 = bf16[1024,1024]{1,0:T(8,128)(2,1)S(1)} copy-done((bf16[1024,1024]{1,0:T(8,128)(2,1)S(1)}, bf16[1024,1024]{1,0:T(8,128)(2,1)}, u32[]{:S(2)}) %copy-start.1) | copy-done | bytes 2097176
  118.3 1.5 %mixed.1 = bf16[256,1024]{1,0:T(8,128)(2,1)} custom-call(bf16[16,2,64,128]{3,2,1,0:T(8,128)(2,1)S(1)} %all-to-all-done.1.att_ref.own_att_ref, bf16[1024,1024]{1,0:T(8,128)(2,1)S(1)} %copy-done.1), custom_call_target="tpu_custom_call" | custom-call | flops 1000000000 | bytes 4194304 | tf_op jit(solution)/shard_map/mixed/pallas_call | solution.py:420
  119.8 0.0 collective-permute-done.4
  119.8 0.7 add_multiply_fusion
  120.5 6.8 %all-to-all-done.2.in_ref = bf16[16,2,192,128]{3,2,1,0:T(8,128)(2,1)S(1)} async-done(((bf16[16,2,192,128]{3,2,1,0:T(8,128)(2,1)}), bf16[16,2,192,128]{3,2,1,0:T(8,128)(2,1)S(1)}, u32[]{:S(2)}, u32[]{:S(2)}) %all-to-all-start.2) | async-done | bytes 1572896 | tf_op jit(solution)/shard_map/all_to_all | solution.py:321
  127.3 1.6 %unpack.1 = (bf16[256,1024]{1,0:T(8,128)(2,1)}, bf16[256,1024]{1,0:T(8,128)(2,1)}, bf16[256,1024]{1,0:T(8,128)(2,1)}) custom-call(bf16[16,2,192,128]{3,2,1,0:T(8,128)(2,1)S(1)} %all-to-all-done.2.in_ref), custom_call_target="tpu_custom_call" | custom-call | bytes 4194304 | tf_op jit(solution)/shard_map/unpack/pallas_call | solution.py:421
  (4 shorter events, 0.0 us)
Async XLA Ops:
  5.2 35.6 %copy-start.3 = (s32[1,32]{1,0:T(1,128)S(1)}, s32[1,32]{1,0:T(1,128)}, u32[]{:S(2)}) copy-start(s32[1,32]{1,0:T(1,128)} %param.13) | copy-start | bytes 388
  5.2 35.6 %copy-start.4 = (s32[1,32,16]{1,2,0:T(8,128)S(1)}, s32[1,32,16]{1,2,0:T(8,128)}, u32[]{:S(2)}) copy-start(s32[1,32,16]{1,2,0:T(8,128)} %param.12) | copy-start | bytes 6148
  5.2 35.6 %copy-start.5 = (s32[32]{0:T(128)S(1)}, s32[32]{0:T(128)}, u32[]{:S(2)}) copy-start(s32[32]{0:T(128)} %get-tuple-element.23.order_ref) | copy-start | bytes 388
  40.8 16.3 %copy-start.2 = (bf16[16,2,256,128]{3,2,1,0:T(8,128)(2,1)}, bf16[16,2,256,128]{3,2,1,0:T(8,128)(2,1)S(1)}, u32[]{:S(2)}) copy-start(bf16[16,2,256,128]{3,2,1,0:T(8,128)(2,1)S(1)} %all_to_all.20) | copy-start | bytes 6291460
  53.4 11.8 %copy-start.7 = (f32[32,8,128]{2,1,0:T(8,128)}, f32[32,8,128]{2,1,0:T(8,128)S(1)}, u32[]{:S(2)}) copy-start(f32[32,8,128]{2,1,0:T(8,128)S(1)} %get-tuple-element.34.stat_ref) | copy-start | bytes 393220
  53.4 14.3 %all-to-all-start.1 = ((bf16[16,2,64,128]{3,2,1,0:T(8,128)(2,1)}), bf16[16,2,64,128]{3,2,1,0:T(8,128)(2,1)S(1)}, u32[]{:S(2)}, u32[]{:S(2)}) async-start(bf16[16,2,64,128]{3,2,1,0:T(8,128)(2,1)} %bitcast.8), calls=%async_computation.1 | async-start | bytes 1048576 | tf_op jit(solution)/shard_map/all_to_all | solution.py:321
  57.1 10.5 %copy-start = (bf16[1,256,1024]{2,1,0:T(8,128)(2,1)S(1)}, bf16[1,256,1024]{2,1,0:T(8,128)(2,1)}, u32[]{:S(2)}) copy-start(bf16[1,256,1024]{2,1,0:T(8,128)(2,1)} %param.10) | copy-start | bytes 1572868
  65.2 1.1 copy-start.6
  67.6 2.3 %collective-permute-start = (bf16[16,2,64,128]{3,2,1,0:T(8,128)(2,1)S(1)}, bf16[16,2,64,128]{3,2,1,0:T(8,128)(2,1)S(1)}, u32[]{:S(2)}, u32[]{:S(2)}) collective-permute-start(bf16[16,2,64,128]{3,2,1,0:T(8,128)(2,1)S(1)} %all-to-all-done.1.att_ref.own_att_ref), channel_id=1, source_target_pairs={{0,16},{16,0},{32,48},{48,32},{64,80},{80,64},{96,112},{112,96},{1... | collective-permute-start | bytes 1572872 | tf_op jit(solution)/shard_map/ppermute | solution.py:382
  67.9 2.1 %collective-permute-start.1 = (bf16[256,512]{1,0:T(8,128)(2,1)S(1)}, bf16[256,512]{1,0:T(8,128)(2,1)S(1)}, u32[]{:S(2)}, u32[]{:S(2)}) collective-permute-start(bf16[256,512]{1,0:T(8,128)(2,1)S(1)} %get-tuple-element.32), channel_id=1, source_target_pairs={{0,16},{16,0},{32,48},{48,32},{64,80},{80,64},{96,112},{112,96},{1... | collective-permute-start | bytes 786440 | tf_op jit(solution)/shard_map/ppermute | solution.py:348
  71.6 23.5 %all-to-all-start.3 = ((bf16[16,64,512]{2,1,0:T(8,128)(2,1)}), bf16[16,64,512]{2,1,0:T(8,128)(2,1)S(1)}, u32[]{:S(2)}, u32[]{:S(2)}) async-start(bf16[16,64,512]{2,1,0:T(8,128)(2,1)} %bitcast.16), calls=%async_computation.3 | async-start | bytes 2097152 | tf_op jit(solution)/shard_map/all_to_all | solution.py:321
  95.1 32.2 %all-to-all-start.2 = ((bf16[16,2,192,128]{3,2,1,0:T(8,128)(2,1)}), bf16[16,2,192,128]{3,2,1,0:T(8,128)(2,1)S(1)}, u32[]{:S(2)}, u32[]{:S(2)}) async-start(bf16[16,2,192,128]{3,2,1,0:T(8,128)(2,1)} %bitcast.29), calls=%async_computation.2 | async-start | bytes 3145728 | tf_op jit(solution)/shard_map/all_to_all | solution.py:321
  102.1 7.9 %collective-permute-start.2 = (bf16[64,256]{1,0:T(8,128)(2,1)S(1)}, bf16[64,256]{1,0:T(8,128)(2,1)S(1)}, u32[]{:S(2)}, u32[]{:S(2)}) collective-permute-start(bf16[64,256]{1,0:T(8,128)(2,1)S(1)} %select_convert_fusion), channel_id=1, source_target_pairs={{0,128},{16,144},{32,160},{48,176},{64,192},{80,208},{96,224},{112... | collective-permute-start | bytes 98312 | tf_op jit(solution)/shard_map/ppermute | solution.py:414
  110.0 4.7 %collective-permute-start.3 = (bf16[64,128]{1,0:T(8,128)(2,1)S(1)}, bf16[64,128]{1,0:T(8,128)(2,1)S(1)}, u32[]{:S(2)}, u32[]{:S(2)}) collective-permute-start(bf16[64,128]{1,0:T(8,128)(2,1)S(1)} %select_convert_fusion.2), channel_id=1, source_target_pairs={{0,64},{16,80},{32,96},{48,112},{64,0},{80,16},{96,32},{112,48},{1... | collective-permute-start | bytes 49160 | tf_op jit(solution)/shard_map/ppermute | solution.py:414
  114.8 5.0 %collective-permute-start.4 = (bf16[64,64]{1,0:T(8,128)(2,1)S(1)}, bf16[64,64]{1,0:T(8,128)(2,1)S(1)}, u32[]{:S(2)}, u32[]{:S(2)}) collective-permute-start(bf16[64,64]{1,0:T(8,128)(2,1)S(1)} %select_convert_fusion.1), channel_id=1, source_target_pairs={{0,32},{16,48},{32,0},{48,16},{64,96},{80,112},{96,64},{112,80},{1... | collective-permute-start | bytes 24584 | tf_op jit(solution)/shard_map/ppermute | solution.py:414
  116.7 1.6 %copy-start.1 = (bf16[1024,1024]{1,0:T(8,128)(2,1)S(1)}, bf16[1024,1024]{1,0:T(8,128)(2,1)}, u32[]{:S(2)}) copy-start(bf16[1024,1024]{1,0:T(8,128)(2,1)} %wo_ref.3) | copy-start | bytes 6291460
